TPU v7x, 1024 devices: a whole 8x8x8 slice. The times are simulated.
1024 devices in a mesh: narrow: 64 (over x, z), wide: 16 (over y, core).
Axes of the slice: x: 8, y: 8, z: 8, core: 2. Of those that a mesh axis runs over, the one named last changes fastest.
Arguments:
- flow_state: float32 [19, 512, 128, 128], P(None, 'narrow', 'wide'), as said below
- thermal_distributions_current: float32 [7, 512, 128, 128], P(None, 'narrow', 'wide'), as said below
- fluid_mask: int32 [512, 128, 128], P('narrow', 'wide'), may hold values 0 or 1
- heat_rate: float32 [512, 128, 128], P('narrow', 'wide'), may hold values from 0.6 to 1.8
- solid_source: float32 [1024, 16, 256], P(('narrow', 'wide')), may hold values from -6 to 6
- cube_uptake_coefficients: float32 [1024], P(('narrow', 'wide')), may hold values from 0.05 to 0.5
- owner_of: int32 [262144, 1], P(('narrow', 'wide')), may hold values from 0 to 63; in each aligned block of 256 rows (0 to 255, 256 to 511, ...) at most 16 rows name the same one
- emitting_grid_site: int32 [262144], P(('narrow', 'wide')), may hold values from 0 to 8191
- target_node: int32 [262144], P(('narrow', 'wide')), may hold values from 0 to 255
Outputs:
- stream_distributions_after: float32 [19, 512, 128, 128], P(None, 'narrow', 'wide')
- thermal_distributions_after: float32 [7, 512, 128, 128], P(None, 'narrow', 'wide')
- cube_warmth_values: float32 [1024, 16, 256], P(('narrow', 'wide'))
Inputs may be any that keep to these rules, and one draw needn't show every extreme that they name: `owner_of`: among one device's 256 rows, each owner is named at most 16 times, and in some device's rows some owner is named exactly 16 times. `flow_state`: populations are positive. `thermal_distributions_current`: populations are positive.
All inputs are finite; a program needn't handle non-finite values. No bound on the sum of `fluid_mask` on one device may be relied on, other than what follows from the above.
Results may differ from a plain program's by a relative error of at most 0.000075.
Values sent between devices are 32-bit elements; how exact they have to be, the bound alone decides.
No kernel may reach another device: no remote copies, remote signals or barrier semaphores. Data moves between devices by JAX's collectives and lax.ppermute only.
A program may use at most 32 MiB of HBM per device.

v0:
```python
import math

import jax
import jax.numpy as jnp
import numpy as np
from jax import lax
from jax.sharding import PartitionSpec as P

flow_velocity = np.array(
    [
        [0, 0, 0],
        [1, 0, 0],
        [-1, 0, 0],
        [0, 1, 0],
        [0, -1, 0],
        [0, 0, 1],
        [0, 0, -1],
        [1, 1, 0],
        [-1, -1, 0],
        [1, -1, 0],
        [-1, 1, 0],
        [1, 0, 1],
        [-1, 0, -1],
        [1, 0, -1],
        [-1, 0, 1],
        [0, 1, 1],
        [0, -1, -1],
        [0, 1, -1],
        [0, -1, 1],
    ],
    dtype=np.int32,
)
flow_opposite = [0, 2, 1, 4, 3, 6, 5, 8, 7, 10, 9, 12, 11, 14, 13, 16, 15, 18, 17]
flow_weight = [1.0 / 3.0] + [1.0 / 18.0] * 6 + [1.0 / 36.0] * 12
thermal_stencil_coefficient = [0.25] + [0.125] * 6
flow_rate = 1.2
interface_exchange = 0.5


def padded_2(block, sides, width):
    for axis, dim in sides:
        count = lax.axis_size(axis)
        forward = [(i, i + 1) for i in range(count - 1)]
        forward.append((count - 1, 0))
        backward = [(target, source) for source, target in forward]
        low = lax.ppermute(
            lax.slice_in_dim(block, block.shape[dim] - width, None, axis=dim), axis, forward
        )
        high = lax.ppermute(lax.slice_in_dim(block, 0, width, axis=dim), axis, backward)
        block = jnp.concatenate([low, block, high], axis=dim)
    return block


def moment(stacked, axis_number):
    running = jnp.zeros_like(stacked[0])
    for speed_coordinate in range(stacked.shape[0]):
        direction = int(flow_velocity[speed_coordinate, axis_number])
        if direction > 0:
            running = running + stacked[speed_coordinate]
        elif direction < 0:
            running = running - stacked[speed_coordinate]
    return running


def collide(flow_state, thermal_distributions_current, fluid_mask, heat_rate):
    density = jnp.sum(flow_state, axis=0)
    speed_x = moment(flow_state, 0) / density
    speed_y = moment(flow_state, 1) / density
    speed_z = moment(flow_state, 2) / density
    square = speed_x * speed_x + speed_y * speed_y + speed_z * speed_z
    is_fluid = fluid_mask == 1
    flow_parts = []
    for speed_coordinate in range(19):
        velocity = flow_velocity[speed_coordinate]
        directional_speed_product = (
            float(velocity[0]) * speed_x
            + float(velocity[1]) * speed_y
            + float(velocity[2]) * speed_z
        )
        balanced_distribution = (
            flow_weight[speed_coordinate]
            * density
            * (
                1.0
                + 3.0 * directional_speed_product
                + 4.5 * directional_speed_product * directional_speed_product
                - 1.5 * square
            )
        )
        relaxed = flow_state[speed_coordinate] - flow_rate * (
            flow_state[speed_coordinate] - balanced_distribution
        )
        flow_parts.append(jnp.where(is_fluid, relaxed, flow_state[flow_opposite[speed_coordinate]]))
    coolant_warmth = jnp.sum(thermal_distributions_current, axis=0)
    heat_parts = []
    for speed_coordinate in range(7):
        velocity = flow_velocity[speed_coordinate]
        directional_speed_product = (
            float(velocity[0]) * speed_x
            + float(velocity[1]) * speed_y
            + float(velocity[2]) * speed_z
        )
        balanced_distribution = (
            thermal_stencil_coefficient[speed_coordinate]
            * coolant_warmth
            * (1.0 + 4.0 * directional_speed_product)
        )
        relaxed = thermal_distributions_current[speed_coordinate] - heat_rate * (
            thermal_distributions_current[speed_coordinate] - balanced_distribution
        )
        heat_parts.append(
            jnp.where(
                is_fluid, relaxed, thermal_distributions_current[flow_opposite[speed_coordinate]]
            )
        )
    return jnp.stack(flow_parts + heat_parts)


def sine_table(size):
    counting = jnp.arange(1, size + 1, dtype=jnp.float32)
    angles = math.pi * counting[:, None] * counting[None, :] / (size + 1)
    eigen_vectors = math.sqrt(2.0 / (size + 1)) * jnp.sin(angles)
    eigen_values = 2.0 - 2.0 * jnp.cos(math.pi * counting / (size + 1))
    return (eigen_vectors, eigen_values)


def compute_cube_diffusion(system_load_vector, cube_uptake_coefficients, size):
    eigen_vectors, eigen_values = sine_table(size)
    blocks = system_load_vector.shape[0]
    block_cube = system_load_vector.reshape(blocks, size, size, size)
    highest = lax.Precision.HIGHEST
    spectral = jnp.einsum("ai,bijk->bajk", eigen_vectors, block_cube, precision=highest)
    spectral = jnp.einsum("aj,bijk->biak", eigen_vectors, spectral, precision=highest)
    spectral = jnp.einsum("ak,bijk->bija", eigen_vectors, spectral, precision=highest)
    denominator = (
        cube_uptake_coefficients[:, None, None, None]
        + eigen_values[None, :, None, None]
        + eigen_values[None, None, :, None]
        + eigen_values[None, None, None, :]
    )
    spectral = spectral / denominator
    spectral = jnp.einsum("ai,bijk->bajk", eigen_vectors, spectral, precision=highest)
    spectral = jnp.einsum("aj,bijk->biak", eigen_vectors, spectral, precision=highest)
    spectral = jnp.einsum("ak,bijk->bija", eigen_vectors, spectral, precision=highest)
    return spectral.reshape(blocks, size, size * size)


def velocity_of(speed_coordinate):
    return flow_velocity[speed_coordinate if speed_coordinate < 19 else speed_coordinate - 19]


def shift_local(padded_one, speed_coordinate, width_x, width_y):
    velocity = velocity_of(speed_coordinate)
    start_x = 1 - int(velocity[0])
    start_y = 1 - int(velocity[1])
    window = padded_one[start_x : start_x + width_x, start_y : start_y + width_y, :]
    return jnp.roll(window, int(velocity[2]), axis=2)


def per_device(
    flow_state,
    thermal_distributions_current,
    fluid_mask,
    heat_rate,
    solid_source,
    cube_uptake_coefficients,
    owner_of,
    emitting_grid_site,
    target_node,
):
    width_x = flow_state.shape[1]
    width_y = flow_state.shape[2]
    depth_z = flow_state.shape[3]
    stacked = collide(flow_state, thermal_distributions_current, fluid_mask, heat_rate)
    padded = padded_2(stacked, (("narrow", 1), ("wide", 2)), 1)
    moved_distributions = [
        shift_local(padded[speed_coordinate], speed_coordinate, width_x, width_y)
        for speed_coordinate in range(26)
    ]
    stream_distributions_after = jnp.stack(moved_distributions[:19])
    thermal_distributions_moved = moved_distributions[19:]
    coolant_warmth = jnp.sum(jnp.stack(thermal_distributions_moved), axis=0)
    peer_count = lax.axis_size("narrow")
    row_count = emitting_grid_site.shape[0]
    capacity = max(4 * row_count // peer_count, 2)
    owners = owner_of[:, 0]
    owner_hits = (owners[:, None] == jnp.arange(peer_count, dtype=jnp.int32)[None, :]).astype(
        jnp.int32
    )
    ranked = jnp.sum(jnp.cumsum(owner_hits, axis=0) * owner_hits, axis=1) - 1
    slot_index = owners * capacity + ranked
    interface_entry_warmth = coolant_warmth.reshape(-1)[emitting_grid_site]
    send_temp = (
        jnp.zeros((peer_count * capacity,), jnp.float32)
        .at[slot_index]
        .set(interface_entry_warmth)
        .reshape(peer_count, capacity)
    )
    send_node = (
        jnp.zeros((peer_count * capacity,), jnp.int32)
        .at[slot_index]
        .set(target_node)
        .reshape(peer_count, capacity)
    )
    arrived_temp, arrived_node = (
        lax.all_to_all(send_temp, "narrow", split_axis=0, concat_axis=0, tiled=True),
        lax.all_to_all(send_node, "narrow", split_axis=0, concat_axis=0, tiled=True),
    )
    arrived_temp = arrived_temp.reshape(-1)
    arrived_node = arrived_node.reshape(-1)
    blocks = solid_source.shape[0]
    block_edge_length = solid_source.shape[1]
    face_size = solid_source.shape[2]
    facet_heating = jax.ops.segment_sum(
        interface_exchange * arrived_temp, arrived_node, num_segments=blocks * face_size
    )
    system_load_vector = solid_source.at[:, 0, :].add(facet_heating.reshape(blocks, face_size))
    cube_warmth_values = compute_cube_diffusion(
        system_load_vector, cube_uptake_coefficients, block_edge_length
    )
    boundary_sites = cube_warmth_values[:, 0, :].reshape(-1)
    slot_flux = interface_exchange * (boundary_sites[arrived_node] - arrived_temp)
    returned = lax.all_to_all(
        slot_flux.reshape(peer_count, capacity), "narrow", split_axis=0, concat_axis=0, tiled=True
    )
    interface_entry_flux = returned.reshape(-1)[slot_index]
    heat_gain = jax.ops.segment_sum(
        interface_entry_flux, emitting_grid_site, num_segments=width_x * width_y * depth_z
    )
    heat_gain = heat_gain.reshape(width_x, width_y, depth_z)
    thermal_distributions_after = jnp.stack(
        [
            thermal_distributions_moved[speed_coordinate]
            + thermal_stencil_coefficient[speed_coordinate] * heat_gain
            for speed_coordinate in range(7)
        ]
    )
    return (stream_distributions_after, thermal_distributions_after, cube_warmth_values)


def solution(mesh):
    return jax.shard_map(
        per_device,
        mesh=mesh,
        in_specs=(
            P(None, "narrow", "wide", None),
            P(None, "narrow", "wide", None),
            P("narrow", "wide", None),
            P("narrow", "wide", None),
            P(("narrow", "wide"), None, None),
            P(("narrow", "wide")),
            P(("narrow", "wide"), None),
            P(("narrow", "wide")),
            P(("narrow", "wide")),
        ),
        out_specs=(
            P(None, "narrow", "wide", None),
            P(None, "narrow", "wide", None),
            P(("narrow", "wide"), None, None),
        ),
        check_vma=False,
    )
```

profile of v0, /device:TPU:49, one launch (start us, length us, event | category | flops | bytes accessed | tf_op | source)
XLA Modules:
  0.0 121.0 jit_solution(13733034607196058059)
XLA Ops:
  0.6 0.8 copy.155
  1.4 1.1 reduce_sum.59
  2.5 1.1 constant_dynamic-update-slice_fusion.25
  3.7 0.8 constant_dynamic-update-slice_fusion.24
  4.5 0.9 constant_dynamic-update-slice_fusion.23
  6.4 4.9 %collective-permute-start = (f32[26,1,8,128]{3,2,1,0:T(8,128)S(1)}, f32[26,1,8,128]{3,2,1,0:T(8,128)S(1)}, u32[]{:S(2)}, u32[]{:S(2)}) collective-permute-start(f32[26,1,8,128]{3,2,1,0:T(8,128)S(1)} %get-tuple-element.61), channel_id=1, source_target_pairs={{0,16},{16,32},{32,48},{48,64},{64,80},{80,96},{96,112},{112,128},... | collective-permute-start | bytes 319496 | tf_op jit(solution)/shard_map/ppermute | solution.py:46
  11.3 16.4 %collective-permute-start.1 = (f32[26,1,8,128]{3,2,1,0:T(8,128)S(1)}, f32[26,1,8,128]{3,2,1,0:T(8,128)S(1)}, u32[]{:S(2)}, u32[]{:S(2)}) collective-permute-start(f32[26,1,8,128]{3,2,1,0:T(8,128)S(1)} %get-tuple-element.62), channel_id=1, source_target_pairs={{16,0},{32,16},{48,32},{64,48},{80,64},{96,80},{112,96},{128,112},... | collective-permute-start | bytes 319496 | tf_op jit(solution)/shard_map/ppermute | solution.py:49
  28.6 1.6 %scatter_custom_fusion = s32[1024]{0:T(1024)S(1)} fusion(s32[256]{0:T(256)S(1)} %bitcast.588, s32[256]{0:T(256)} %param.19, s32[]{:T(128)} %constant.84.clone.1), kind=kCustom, calls=%fused_computation.418 | custom fusion | bytes 4608 | tf_op jit(solution)/shard_map/scatter | solution.py:202
  30.9 6.4 %all-to-all-start = ((s32[64,1,16]{2,1,0:T(1,128)}), s32[64,1,16]{2,1,0:T(1,128)S(1)}, u32[]{:S(2)}, u32[]{:S(2)}) async-start(s32[64,1,16]{2,1,0:T(1,128)} %bitcast.96), calls=%async_computation | async-start | bytes 65536 | tf_op jit(solution)/shard_map/all_to_all | solution.py:207
  38.2 9.9 %all-to-all-done = s32[64,1,16]{2,1,0:T(1,128)S(1)} async-done(((s32[64,1,16]{2,1,0:T(1,128)}), s32[64,1,16]{2,1,0:T(1,128)S(1)}, u32[]{:S(2)}, u32[]{:S(2)}) %all-to-all-start) | async-done | bytes 4128 | tf_op jit(solution)/shard_map/all_to_all | solution.py:207
  49.6 5.2 %collective-permute-start.2 = (f32[26,10,1,128]{3,2,1,0:T(1,128)S(1)}, f32[26,10,1,128]{3,2,1,0:T(1,128)S(1)}, u32[]{:S(2)}, u32[]{:S(2)}) collective-permute-start(f32[26,10,1,128]{3,2,1,0:T(1,128)S(1)} %get-tuple-element.59), channel_id=1, source_target_pairs={{0,1},{1,2},{2,3},{3,4},{4,5},{5,6},{6,7},{7,8},{8,9},{9,10},{10,1... | collective-permute-start | bytes 399368 | tf_op jit(solution)/shard_map/ppermute | solution.py:46
  54.8 2.0 %collective-permute-done.2 = f32[26,10,1,128]{3,2,1,0:T(1,128)S(1)} collective-permute-done((f32[26,10,1,128]{3,2,1,0:T(1,128)S(1)}, f32[26,10,1,128]{3,2,1,0:T(1,128)S(1)}, u32[]{:S(2)}, u32[]{:S(2)}) %collective-permute-start.2) | collective-permute-done | bytes 133152 | tf_op jit(solution)/shard_map/ppermute | solution.py:46
  56.8 3.7 %collective-permute-done.3 = f32[26,10,1,128]{3,2,1,0:T(1,128)S(1)} collective-permute-done((f32[26,10,1,128]{3,2,1,0:T(1,128)S(1)}, f32[26,10,1,128]{3,2,1,0:T(1,128)S(1)}, u32[]{:S(2)}, u32[]{:S(2)}) %collective-permute-start.3) | collective-permute-done | bytes 133152 | tf_op jit(solution)/shard_map/ppermute | solution.py:49
  61.5 1.7 %gather_fusion = f32[256]{0:T(256)S(1)} fusion(f32[8192]{0:T(1024)S(1)} %fusion.155, s32[1024]{0:T(1024)S(1)} %pad_clamp_fusion.1), kind=kCustom, calls=%fused_computation | custom fusion | bytes 3072 | tf_op jit(solution)/shard_map/gather | solution.py:192
  63.2 1.4 %scatter_custom_fusion.1 = f32[1024]{0:T(1024)S(1)} fusion(s32[256]{0:T(256)S(1)} %bitcast.590, f32[256]{0:T(256)S(1)} %gather_fusion, f32[]{:T(128)} %constant.35.clone.1), kind=kCustom, calls=%fused_computation.416 | custom fusion | bytes 4100 | tf_op jit(solution)/shard_map/scatter | solution.py:196
  65.3 4.6 %all-to-all-start.1 = ((f32[64,1,16]{2,1,0:T(1,128)}), f32[64,1,16]{2,1,0:T(1,128)S(1)}, u32[]{:S(2)}, u32[]{:S(2)}) async-start(f32[64,1,16]{2,1,0:T(1,128)} %bitcast.104), calls=%async_computation.1 | async-start | bytes 65536 | tf_op jit(solution)/shard_map/all_to_all | solution.py:206
  70.2 10.5 %all-to-all-done.1 = f32[64,1,16]{2,1,0:T(1,128)S(1)} async-done(((f32[64,1,16]{2,1,0:T(1,128)}), f32[64,1,16]{2,1,0:T(1,128)S(1)}, u32[]{:S(2)}, u32[]{:S(2)}) %all-to-all-start.1) | async-done | bytes 4128 | tf_op jit(solution)/shard_map/all_to_all | solution.py:206
  80.9 7.6 %scatter_custom_fusion.2 = f32[256]{0:T(256)S(1)} fusion(s32[1024]{0:T(1024)S(1)} %reshape.378, f32[1024]{0:T(1024)S(1)} %reshape.380, f32[]{:T(128)} %constant.35.clone.1), kind=kCustom, calls=%fused_computation.424 | custom fusion | flops 1024 | bytes 1028 | tf_op jit(solution)/shard_map/scatter-add | solution.py:214
  91.5 6.8 %gather_fusion.1 = f32[1024]{0:T(1024)S(1)} fusion(f32[256]{0:T(256)S(1)} %bitcast.582, s32[1024]{0:T(1024)S(1)} %broadcast_clamp_fusion), kind=kCustom, calls=%fused_computation.1 | custom fusion | bytes 12288 | tf_op jit(solution)/shard_map/gather | solution.py:222
  99.2 4.6 %all-to-all-start.2 = ((f32[64,1,16]{2,1,0:T(1,128)}), f32[64,1,16]{2,1,0:T(1,128)S(1)}, u32[]{:S(2)}, u32[]{:S(2)}) async-start(f32[64,1,16]{2,1,0:T(1,128)} %copy.95), calls=%async_computation.2 | async-start | bytes 65536 | tf_op jit(solution)/shard_map/all_to_all | solution.py:223
  104.6 10.0 %all-to-all-done.2 = f32[64,1,16]{2,1,0:T(1,128)S(1)} async-done(((f32[64,1,16]{2,1,0:T(1,128)}), f32[64,1,16]{2,1,0:T(1,128)S(1)}, u32[]{:S(2)}, u32[]{:S(2)}) %all-to-all-start.2) | async-done | bytes 4128 | tf_op jit(solution)/shard_map/all_to_all | solution.py:223
  115.9 1.4 %gather_fusion.2 = f32[256]{0:T(256)S(1)} fusion(f32[1024]{0:T(1024)S(1)} %reshape.333, s32[1024]{0:T(1024)S(1)} %pad_clamp_fusion), kind=kCustom, calls=%fused_computation.2 | custom fusion | bytes 3072 | tf_op jit(solution)/shard_map/gather | solution.py:226
  117.3 2.0 %scatter_custom_fusion.3 = f32[8192]{0:T(1024)S(1)} fusion(s32[256]{0:T(256)S(1)} %copy-done.7, f32[256]{0:T(256)S(1)} %gather_fusion.2, f32[]{:T(128)} %constant.35.clone.1), kind=kCustom, calls=%fused_computation.372 | custom fusion | flops 256 | bytes 32772 | tf_op jit(solution)/shard_map/scatter-add | solution.py:227
  120.2 0.8 copy-done.6
  (146 shorter events, 13.1 us)
Async XLA Ops:
  0.6 4.7 %copy-start = (f32[19,8,8,128]{3,2,1,0:T(8,128)S(1)}, f32[19,8,8,128]{3,2,1,0:T(8,128)}, u32[]{:S(2)}) copy-start(f32[19,8,8,128]{3,2,1,0:T(8,128)} %param.11) | copy-start | bytes 1867780
  4.5 1.5 %copy-start.1 = (f32[7,8,8,128]{3,2,1,0:T(8,128)S(1)}, f32[7,8,8,128]{3,2,1,0:T(8,128)}, u32[]{:S(2)}) copy-start(f32[7,8,8,128]{3,2,1,0:T(8,128)} %param.12) | copy-start | bytes 688132
  5.4 0.8 copy-start.2
  5.7 22.0 %copy-start.4 = (s32[256,1]{0,1:T(1,128)S(1)}, s32[256,1]{0,1:T(1,128)}, u32[]{:S(2)}) copy-start(s32[256,1]{0,1:T(1,128)} %param.17) | copy-start | bytes 3076
  5.7 31.6 %copy-start.7 = (s32[256]{0:T(256)S(1)}, s32[256]{0:T(256)}, u32[]{:S(2)}) copy-start(s32[256]{0:T(256)} %param.18) | copy-start | bytes 3076
  6.4 43.1 %collective-permute-start = (f32[26,1,8,128]{3,2,1,0:T(8,128)S(1)}, f32[26,1,8,128]{3,2,1,0:T(8,128)S(1)}, u32[]{:S(2)}, u32[]{:S(2)}) collective-permute-start(f32[26,1,8,128]{3,2,1,0:T(8,128)S(1)} %get-tuple-element.61), channel_id=1, source_target_pairs={{0,16},{16,32},{32,48},{48,64},{64,80},{80,96},{96,112},{112,128},... | collective-permute-start | bytes 319496 | tf_op jit(solution)/shard_map/ppermute | solution.py:46
  11.3 38.2 %collective-permute-start.1 = (f32[26,1,8,128]{3,2,1,0:T(8,128)S(1)}, f32[26,1,8,128]{3,2,1,0:T(8,128)S(1)}, u32[]{:S(2)}, u32[]{:S(2)}) collective-permute-start(f32[26,1,8,128]{3,2,1,0:T(8,128)S(1)} %get-tuple-element.62), channel_id=1, source_target_pairs={{16,0},{32,16},{48,32},{64,48},{80,64},{96,80},{112,96},{128,112},... | collective-permute-start | bytes 319496 | tf_op jit(solution)/shard_map/ppermute | solution.py:49
  30.9 17.1 %all-to-all-start = ((s32[64,1,16]{2,1,0:T(1,128)}), s32[64,1,16]{2,1,0:T(1,128)S(1)}, u32[]{:S(2)}, u32[]{:S(2)}) async-start(s32[64,1,16]{2,1,0:T(1,128)} %bitcast.96), calls=%async_computation | async-start | bytes 65536 | tf_op jit(solution)/shard_map/all_to_all | solution.py:207
  49.6 7.2 %collective-permute-start.2 = (f32[26,10,1,128]{3,2,1,0:T(1,128)S(1)}, f32[26,10,1,128]{3,2,1,0:T(1,128)S(1)}, u32[]{:S(2)}, u32[]{:S(2)}) collective-permute-start(f32[26,10,1,128]{3,2,1,0:T(1,128)S(1)} %get-tuple-element.59), channel_id=1, source_target_pairs={{0,1},{1,2},{2,3},{3,4},{4,5},{5,6},{6,7},{7,8},{8,9},{9,10},{10,1... | collective-permute-start | bytes 399368 | tf_op jit(solution)/shard_map/ppermute | solution.py:46
  54.8 5.6 %collective-permute-start.3 = (f32[26,10,1,128]{3,2,1,0:T(1,128)S(1)}, f32[26,10,1,128]{3,2,1,0:T(1,128)S(1)}, u32[]{:S(2)}, u32[]{:S(2)}) collective-permute-start(f32[26,10,1,128]{3,2,1,0:T(1,128)S(1)} %get-tuple-element.60), channel_id=1, source_target_pairs={{1,0},{2,1},{3,2},{4,3},{5,4},{6,5},{7,6},{8,7},{9,8},{10,9},{11,1... | collective-permute-start | bytes 399368 | tf_op jit(solution)/shard_map/ppermute | solution.py:49
  65.3 15.3 %all-to-all-start.1 = ((f32[64,1,16]{2,1,0:T(1,128)}), f32[64,1,16]{2,1,0:T(1,128)S(1)}, u32[]{:S(2)}, u32[]{:S(2)}) async-start(f32[64,1,16]{2,1,0:T(1,128)} %bitcast.104), calls=%async_computation.1 | async-start | bytes 65536 | tf_op jit(solution)/shard_map/all_to_all | solution.py:206
  91.5 7.0 %copy-start.3 = (f32[1,16,256]{2,1,0:T(8,128)}, f32[1,16,256]{2,1,0:T(8,128)S(1)}, u32[]{:S(2)}) copy-start(f32[1,16,256]{2,1,0:T(8,128)S(1)} %reshape.332) | copy-start | bytes 49156
  99.2 15.3 %all-to-all-start.2 = ((f32[64,1,16]{2,1,0:T(1,128)}), f32[64,1,16]{2,1,0:T(1,128)S(1)}, u32[]{:S(2)}, u32[]{:S(2)}) async-start(f32[64,1,16]{2,1,0:T(1,128)} %copy.95), calls=%async_computation.2 | async-start | bytes 65536 | tf_op jit(solution)/shard_map/all_to_all | solution.py:223
  119.5 0.7 copy-start.5
  120.2 0.8 copy-start.6
where the time goes:
time: 122 us; the launch traced here: 121 us
  starting transfers between devices  42 us (34%)
  waiting for transfers between devices  36 us (30%)
  local copies, waits for them, and re-layouts  20.5 us (17%)
  other arithmetic  18.3 us (15%)
  matrix products  2.3 us (2%)
  between operations  1.95 us (2%)
    ppermute x2, starting transfers between devices, padded_2(): lax.ppermute(lax.slice_in_dim(block, 0, width, axis=dim), axis, backward)  16.4 us
    all_to_all x1, waiting for transfers between devices, per_device(): lax.all_to_all(send_temp, 'narrow', split_axis=0, concat_axis=0, tiled=True)  10.5 us
    ppermute x2, starting transfers between devices, padded_2(): lax.ppermute(lax.slice_in_dim(block, block.shape[dim] - width, None, axis...  10.1 us
    all_to_all x1, waiting for transfers between devices, per_device(): lax.all_to_all(slot_flux.reshape(peer_count, capacity), 'narrow', split_a...  10 us
    all_to_all x1, waiting for transfers between devices, per_device(): lax.all_to_all(send_node, 'narrow', split_axis=0, concat_axis=0, tiled=True)  9.88 us
    scatter-add x1, other arithmetic, per_device(): jax.ops.segment_sum(interface_exchange * arrived_temp, arrived_node, num_...  7.62 us
    gather x3, local copies, waits for them, and re-layouts, per_device(): boundary_sites[arrived_node] - arrived_temp  6.97 us
    all_to_all x1, starting transfers between devices, per_device(): lax.all_to_all(send_node, 'narrow', split_axis=0, concat_axis=0, tiled=True)  6.35 us
  transfers between devices with their start and end apart: 7, of which 5 were waited for; matrix products, arithmetic and copies ran while one was open for 4% of the time, Pallas kernels for 0%

commit v1 on v0

v1 whole, which is shorter than its diff:
```python
import functools
import math

import jax
import jax.numpy as jnp
import numpy as np
from jax import lax
from jax.experimental import pallas as pl
from jax.experimental.pallas import tpu as pltpu
from jax.sharding import PartitionSpec as P

flow_velocity = np.array(
    [
        [0, 0, 0],
        [1, 0, 0],
        [-1, 0, 0],
        [0, 1, 0],
        [0, -1, 0],
        [0, 0, 1],
        [0, 0, -1],
        [1, 1, 0],
        [-1, -1, 0],
        [1, -1, 0],
        [-1, 1, 0],
        [1, 0, 1],
        [-1, 0, -1],
        [1, 0, -1],
        [-1, 0, 1],
        [0, 1, 1],
        [0, -1, -1],
        [0, 1, -1],
        [0, -1, 1],
    ],
    dtype=np.int32,
)
flow_opposite = [0, 2, 1, 4, 3, 6, 5, 8, 7, 10, 9, 12, 11, 14, 13, 16, 15, 18, 17]
flow_weight = [1.0 / 3.0] + [1.0 / 18.0] * 6 + [1.0 / 36.0] * 12
thermal_stencil_coefficient = [0.25] + [0.125] * 6
flow_rate = 1.2
interface_exchange = 0.5

x_up = (1, 7, 9, 11, 13)
x_down = (2, 8, 10, 12, 14)
y_up = (3, 15, 17)
y_down = (4, 16, 18)
diagonal_up = (7, 10)
diagonal_down = (8, 9)

HIGHEST = lax.Precision.HIGHEST
params = pltpu.CompilerParams(vmem_limit_bytes=32 * 1024 * 1024)


def sine_constants(size):
    counting = np.arange(1, size + 1, dtype=np.float64)
    sine = math.sqrt(2.0 / (size + 1)) * np.sin(
        math.pi * counting[:, None] * counting[None, :] / (size + 1)
    )
    values = 2.0 - 2.0 * np.cos(math.pi * counting / (size + 1))
    plane = np.kron(sine, sine)
    total = values[:, None] + (values[:, None] + values[None, :]).reshape(1, -1)
    return (
        sine.astype(np.float32),
        plane.astype(np.float32),
        total.astype(np.float32),
        np.ascontiguousarray(np.broadcast_to(sine[:, :1], total.shape)).astype(np.float32),
    )


def dot(a, b, precision=None):
    return lax.dot_general(
        a, b, (((1,), (0,)), ((), ())), precision=precision, preferred_element_type=jnp.float32
    )


def dot_last(a, b):
    return lax.dot_general(a, b, (((1,), (1,)), ((), ())), preferred_element_type=jnp.float32)


def parts_of(value, count):
    parts = []
    for _ in range(count):
        part = value.astype(jnp.bfloat16)
        parts.append(part)
        value = value - part.astype(jnp.float32)
    return parts


def one_hot(row, size):
    numbers = lax.broadcasted_iota(jnp.int32, (size, row.shape[1]), 0)
    return jnp.where(numbers == row, 1.0, 0.0).astype(jnp.bfloat16)


def collide_kernel(
    flow_ref, heat_ref, mask_ref, rate_ref,
    post_ref, heat_post_ref, xu_ref, xd_ref, yu_ref, yd_ref, du_ref, dd_ref,
):
    wide_x, wide_y = flow_ref.shape[1], flow_ref.shape[2]
    for x in range(wide_x):
        f = [flow_ref[i, x] for i in range(19)]
        density = functools.reduce(lambda a, b: a + b, f)
        momentum = []
        for axis in range(3):
            plus = [f[i] for i in range(19) if flow_velocity[i, axis] > 0]
            minus = [f[i] for i in range(19) if flow_velocity[i, axis] < 0]
            momentum.append(
                functools.reduce(lambda a, b: a + b, plus)
                - functools.reduce(lambda a, b: a + b, minus)
            )
        inverse = 1.0 / density
        speed = [m * inverse for m in momentum]
        square = speed[0] * speed[0] + speed[1] * speed[1] + speed[2] * speed[2]
        base = 1.0 - 1.5 * square
        is_fluid = mask_ref[x] == 1

        def along(i):
            total = None
            for axis in range(3):
                c = int(flow_velocity[i, axis])
                if c == 0:
                    continue
                term = speed[axis] if c > 0 else -speed[axis]
                total = term if total is None else total + term
            return total

        weighted = {w: density * w for w in set(flow_weight)}
        post = [None] * 19
        for i in [0] + list(range(1, 19, 2)):
            scale = weighted[flow_weight[i]]
            if i == 0:
                post[0] = jnp.where(is_fluid, f[0] - flow_rate * (f[0] - scale * base), f[0])
                continue
            cu = along(i)
            even = base + 4.5 * (cu * cu)
            odd = 3.0 * cu
            for k, balanced in ((i, scale * (even + odd)), (i + 1, scale * (even - odd))):
                post[k] = jnp.where(
                    is_fluid, f[k] - flow_rate * (f[k] - balanced), f[flow_opposite[k]]
                )
        h = [heat_ref[i, x] for i in range(7)]
        warmth = functools.reduce(lambda a, b: a + b, h)
        rate = rate_ref[x]
        heat = []
        for i in range(7):
            scale = thermal_stencil_coefficient[i] * warmth
            balanced = scale if i == 0 else scale * (1.0 + 4.0 * along(i))
            heat.append(jnp.where(is_fluid, h[i] - rate * (h[i] - balanced), h[flow_opposite[i]]))
        for i in range(19):
            post_ref[i, x] = post[i]
        for i in range(7):
            heat_post_ref[i, x] = heat[i]
        if x == wide_x - 1:
            for slot, part in enumerate([heat[1]] + [post[i] for i in x_up]):
                xu_ref[slot] = part
        if x == 0:
            for slot, part in enumerate([heat[2]] + [post[i] for i in x_down]):
                xd_ref[slot] = part
        last, row = slice(wide_y - 1, wide_y), slice(x, x + 1)
        for slot, part in enumerate([heat[3]] + [post[i] for i in y_up]):
            yu_ref[slot, row, :] = part[last]
        for slot, part in enumerate([heat[4]] + [post[i] for i in y_down]):
            yd_ref[slot, row, :] = part[0:1]
        for slot, i in enumerate(diagonal_up):
            du_ref[slot, row, :] = post[i][last]
        for slot, i in enumerate(diagonal_down):
            dd_ref[slot, row, :] = post[i][0:1]


def block_kernel(
    source_ref, uptake_ref, sine_ref, plane_ref, total_ref, first_ref, cube_ref, reply_ref
):
    sine, plane = sine_ref[...], plane_ref[...]
    inverse = 1.0 / (total_ref[...] + uptake_ref[0])
    spectral = dot(dot(sine, source_ref[0], HIGHEST), plane, HIGHEST) * inverse
    cube_ref[...] = dot(dot(sine, spectral, HIGHEST), plane, HIGHEST)
    reply_ref[...] = dot(sine, first_ref[...] * inverse, HIGHEST)


def shifted_y(value, direction, edge):
    size = value.shape[0]
    rows = lax.broadcasted_iota(jnp.int32, value.shape, 0)
    if direction > 0:
        return jnp.where(rows == 0, edge, pltpu.roll(value, 1, 0))
    return jnp.where(rows == size - 1, edge, pltpu.roll(value, size - 1, 0))


def shifted_z(value, direction):
    if direction == 0:
        return value
    return pltpu.roll(value, 1 if direction > 0 else value.shape[1] - 1, 1)


def site_one_hots(site_ref, planes, depth):
    rows = site_ref[...]
    row = jnp.concatenate([rows[0:1], rows[1:2]], axis=1)
    return one_hot(row // depth, planes), one_hot(row % depth, depth)


def warmth_kernel(
    heat_post_ref, xu_ref, xd_ref, yu_ref, yd_ref, du_ref, dd_ref,
    site_ref, owner_ref, node_ref, wide_ref, cube_ref, reply_ref,
    passed_ref, warmth_ref, send_ref, du_out_ref, dd_out_ref, *, n_wide, face,
):
    wide_x, wide_y, depth = heat_post_ref.shape[1:]
    planes = []
    for x in range(wide_x):
        passed = [
            heat_post_ref[0, x],
            xu_ref[0] if x == 0 else heat_post_ref[1, x - 1],
            xd_ref[0] if x == wide_x - 1 else heat_post_ref[2, x + 1],
            shifted_y(heat_post_ref[3, x], 1, yu_ref[0, x : x + 1, :]),
            shifted_y(heat_post_ref[4, x], -1, yd_ref[0, x : x + 1, :]),
            shifted_z(heat_post_ref[5, x], 1),
            shifted_z(heat_post_ref[6, x], -1),
        ]
        for i in range(7):
            passed_ref[i, x] = passed[i]
        planes.append(functools.reduce(lambda a, b: a + b, passed))
    field = jnp.concatenate(planes, axis=0)
    count = wide_x * wide_y
    at_plane, at_depth = site_one_hots(site_ref, count, depth)
    picked = dot(jnp.concatenate(parts_of(field, 3), axis=0), at_depth)
    picked = picked[0:count] + picked[count : 2 * count] + picked[2 * count :]
    warmth = jnp.sum(picked * at_plane.astype(jnp.float32), axis=0, keepdims=True)
    warmth_ref[...] = warmth
    number = ((owner_ref[...] * n_wide + wide_ref[0]) * face + node_ref[...]).astype(jnp.float32)
    half = face // 2
    message = jnp.concatenate(
        [
            warmth[:, 0:half], warmth[:, half:], number,
            cube_ref[0:1, 0:half], cube_ref[0:1, half:],
            reply_ref[0:1, 0:half], reply_ref[0:1, half:],
        ],
        axis=0,
    )
    for peer in range(send_ref.shape[0]):
        send_ref[peer] = message
    for slot, i in enumerate(diagonal_up):
        rows = lax.broadcasted_iota(jnp.int32, (wide_x, depth), 0)
        if flow_velocity[i, 0] > 0:
            edge = xu_ref[1 + x_up.index(i), wide_y - 1 : wide_y, :]
            du_out_ref[slot] = jnp.where(rows == 0, edge, pltpu.roll(du_ref[slot], 1, 0))
        else:
            edge = xd_ref[1 + x_down.index(i), wide_y - 1 : wide_y, :]
            du_out_ref[slot] = jnp.where(
                rows == wide_x - 1, edge, pltpu.roll(du_ref[slot], wide_x - 1, 0)
            )
    for slot, i in enumerate(diagonal_down):
        rows = lax.broadcasted_iota(jnp.int32, (wide_x, depth), 0)
        if flow_velocity[i, 0] > 0:
            edge = xu_ref[1 + x_up.index(i), 0:1, :]
            dd_out_ref[slot] = jnp.where(rows == 0, edge, pltpu.roll(dd_ref[slot], 1, 0))
        else:
            edge = xd_ref[1 + x_down.index(i), 0:1, :]
            dd_out_ref[slot] = jnp.where(
                rows == wide_x - 1, edge, pltpu.roll(dd_ref[slot], wide_x - 1, 0)
            )


def stream_kernel(post_ref, xu_ref, xd_ref, yu_ref, yd_ref, du_ref, dd_ref, out_ref):
    wide_x = post_ref.shape[1]
    for i in range(19):
        cx, cy, cz = (int(c) for c in flow_velocity[i])
        for x in range(wide_x):
            if cx > 0 and x == 0:
                value = xu_ref[1 + x_up.index(i)]
            elif cx < 0 and x == wide_x - 1:
                value = xd_ref[1 + x_down.index(i)]
            else:
                value = post_ref[i, x - cx]
            if cy:
                if cx:
                    edges = du_ref if cy > 0 else dd_ref
                    slot = (diagonal_up if cy > 0 else diagonal_down).index(i)
                else:
                    edges = yu_ref if cy > 0 else yd_ref
                    slot = 1 + (y_up if cy > 0 else y_down).index(i)
                value = shifted_y(value, cy, edges[slot, x : x + 1, :])
            out_ref[i, x] = shifted_z(value, cz)


def finish_kernel(
    got_ref, passed_ref, warmth_ref, site_ref, owner_ref, node_ref, me_ref, cube_ref, reply_ref,
    plane_ref, heat_ref, cube_out_ref, high_ref, low_ref, owner_rows_ref, node_rows_ref, table_ref,
    *, n_wide, face,
):
    peers, depth = got_ref.shape[0] // 8, got_ref.shape[1]
    wide_x, wide_y = passed_ref.shape[1:3]
    bits = lambda row: got_ref[pl.ds(row, peers, stride=8), :]
    for half in range(2):
        temperature = bits(half)
        high = temperature.astype(jnp.bfloat16).astype(jnp.float32)
        high_ref[half] = high
        low_ref[half] = temperature - high
        number = bits(2 + half).astype(jnp.int32)
        owner_rows_ref[half] = (number // (n_wide * face)).astype(jnp.float32)
        node_rows_ref[half] = (number % face).astype(jnp.float32)

    def spread(ref, half, d):
        row = ref[half, pl.ds(d, 1), :]
        return jnp.broadcast_to(row, (16, depth)).astype(jnp.bfloat16)

    numbers = lax.broadcasted_iota(jnp.int32, (16, depth), 0).astype(jnp.float32)
    zero = jnp.zeros((16, depth), jnp.bfloat16)
    one = jnp.ones((16, depth), jnp.bfloat16)
    owner_groups = -(-peers // 16)

    def step(block, total):
        left, right = [], []
        for inner in range(unroll):
            d = block * unroll + inner
            for half in range(2):
                node, owner = spread(node_rows_ref, half, d), spread(owner_rows_ref, half, d)
                high, low = spread(high_ref, half, d), spread(low_ref, half, d)
                wanted = [(numbers + 16.0 * g).astype(jnp.bfloat16) for g in range(face // 16)]
                right.append(
                    jnp.concatenate([jnp.where(node == w, one, zero) for w in wanted], axis=0)
                )
                hits = [owner == wanted[g] for g in range(owner_groups)]
                left.append(
                    jnp.concatenate(
                        [jnp.where(hit, high, zero) for hit in hits]
                        + [jnp.where(hit, low, zero) for hit in hits],
                        axis=0,
                    )
                )
        return total + dot_last(
            jnp.concatenate(left, axis=1), jnp.concatenate(right, axis=1)
        )

    unroll = math.gcd(peers, 8)
    both = lax.fori_loop(
        0, peers // unroll, step, jnp.zeros((2 * 16 * owner_groups, face), jnp.float32)
    )
    table = interface_exchange * (both[0:peers] + both[16 * owner_groups :][0:peers])
    plane = plane_ref[...]
    spectral = dot(table, plane, HIGHEST)
    table_ref[...] = spectral
    reply = jnp.concatenate([bits(6), bits(7)], axis=1)
    own = table_ref[pl.ds(me_ref[0], 1), :]
    answers = dot(
        jnp.concatenate([spectral * reply, reply_ref[...] * own], axis=0), plane, HIGHEST
    )
    surface = answers[0:peers] + jnp.concatenate([bits(4), bits(5)], axis=1)
    cube_out_ref[0] = cube_ref[...] + answers[peers:]

    owners, nodes = owner_ref[...], node_ref[...]
    at_owner = one_hot(jnp.concatenate([owners[0:1], owners[1:2]], axis=1), peers)
    at_node = one_hot(jnp.concatenate([nodes[0:1], nodes[1:2]], axis=1), face)
    picked = dot(jnp.concatenate(parts_of(surface, 3), axis=0), at_node)
    picked = picked[0:peers] + picked[peers : 2 * peers] + picked[2 * peers :]
    boundary = jnp.sum(picked * at_owner.astype(jnp.float32), axis=0, keepdims=True)
    flux = interface_exchange * (boundary - warmth_ref[...])
    count = wide_x * wide_y
    at_plane, at_depth = site_one_hots(site_ref, count, depth)
    flux_parts = [
        at_plane * jnp.broadcast_to(part, at_plane.shape) for part in parts_of(flux, 3)
    ]
    gain = dot_last(jnp.concatenate(flux_parts, axis=0), at_depth)
    gain = gain[0:count] + gain[count : 2 * count] + gain[2 * count :]
    for x in range(wide_x):
        rows = gain[x * wide_y : (x + 1) * wide_y]
        for i in range(7):
            heat_ref[i, x] = passed_ref[i, x] + thermal_stencil_coefficient[i] * rows


def call(kernel, shapes, *operands, smem=(), scratch=(), cost=1000000):
    specs = [
        pl.BlockSpec(memory_space=pltpu.SMEM if i in smem else pltpu.VMEM)
        for i in range(len(operands))
    ]
    out_specs = [pl.BlockSpec(memory_space=pltpu.VMEM) for _ in shapes]
    moved = sum(4 * math.prod(o.shape) for o in list(operands) + list(shapes))
    return pl.pallas_call(
        kernel,
        out_shape=list(shapes),
        in_specs=specs,
        out_specs=out_specs,
        scratch_shapes=list(scratch),
        compiler_params=params,
        cost_estimate=pl.CostEstimate(flops=cost, bytes_accessed=moved, transcendentals=0),
    )(*operands)


def f32(*shape):
    return jax.ShapeDtypeStruct(shape, jnp.float32)


def per_device(
    flow_state,
    thermal_distributions_current,
    fluid_mask,
    heat_rate,
    solid_source,
    cube_uptake_coefficients,
    owner_of,
    emitting_grid_site,
    target_node,
):
    bx, by, nz = fluid_mask.shape
    size, face = solid_source.shape[1:]
    peers, n_wide = lax.axis_size("narrow"), lax.axis_size("wide")
    rows = emitting_grid_site.shape[0]
    site = emitting_grid_site.reshape(2, rows // 2)
    owner = owner_of.reshape(2, rows // 2)
    node = target_node.reshape(2, rows // 2)
    me = lax.axis_index("narrow").astype(jnp.int32).reshape(1)
    wide = lax.axis_index("wide").astype(jnp.int32).reshape(1)
    sine, plane, total, first = (jnp.asarray(c) for c in sine_constants(size))

    post, heat_post, xu, xd, yu, yd, du, dd = call(
        collide_kernel,
        (
            f32(19, bx, by, nz), f32(7, bx, by, nz), f32(6, by, nz), f32(6, by, nz),
            f32(4, bx, nz), f32(4, bx, nz), f32(2, bx, nz), f32(2, bx, nz),
        ),
        flow_state, thermal_distributions_current, fluid_mask, heat_rate,
    )
    cube, reply = call(
        block_kernel,
        (f32(size, face), f32(size, face)),
        solid_source, cube_uptake_coefficients, sine, plane, total, first,
        smem=(1,),
    )

    def send(block, axis, step):
        count = lax.axis_size(axis)
        return lax.ppermute(block, axis, [(i, (i + step) % count) for i in range(count)])

    xu, xd = send(xu, "narrow", 1), send(xd, "narrow", -1)
    yu, yd = send(yu, "wide", 1), send(yd, "wide", -1)
    passed, warmth, message, du, dd = call(
        functools.partial(warmth_kernel, n_wide=n_wide, face=face),
        (
            f32(7, bx, by, nz), f32(1, rows), f32(peers, 8, face // 2),
            f32(2, bx, nz), f32(2, bx, nz),
        ),
        heat_post, xu, xd, yu, yd, du, dd, site, owner, node, wide, cube, reply,
        smem=(10,),
    )
    got = lax.all_to_all(message, "narrow", split_axis=0, concat_axis=0, tiled=True)
    du, dd = send(du, "wide", 1), send(dd, "wide", -1)
    (stream,) = call(
        stream_kernel, (f32(19, bx, by, nz),), post, xu, xd, yu, yd, du, dd
    )
    heat, cubes = call(
        functools.partial(finish_kernel, n_wide=n_wide, face=face),
        (f32(7, bx, by, nz), f32(1, size, face)),
        got.reshape(peers * 8, face // 2), passed, warmth, site, owner, node, me, cube, reply,
        plane,
        smem=(6,),
        scratch=[pltpu.VMEM((2, peers, face // 2), jnp.float32)] * 4
        + [pltpu.VMEM((peers, face), jnp.float32)],
    )
    return stream, heat, cubes


def solution(mesh):
    return jax.shard_map(
        per_device,
        mesh=mesh,
        in_specs=(
            P(None, "narrow", "wide", None),
            P(None, "narrow", "wide", None),
            P("narrow", "wide", None),
            P("narrow", "wide", None),
            P(("narrow", "wide"), None, None),
            P(("narrow", "wide")),
            P(("narrow", "wide"), None),
            P(("narrow", "wide")),
            P(("narrow", "wide")),
        ),
        out_specs=(
            P(None, "narrow", "wide", None),
            P(None, "narrow", "wide", None),
            P(("narrow", "wide"), None, None),
        ),
        check_vma=False,
    )
```

time: 122 us -> 61.2 us (0.50)
  waiting for transfers between devices: 36 us -> 14.4 us
  other arithmetic: 18.3 us -> 0 us
  local copies, waits for them, and re-layouts: 20.5 us -> 4.28 us
  starting transfers between devices: 42 us -> 31.9 us
  Pallas kernels: 0 us -> 8.8 us
  matrix products: 2.3 us -> 0 us
    all_to_all x3 -> x1, waiting for transfers between devices: 30.4 us -> 7.01 us  [per_device(): lax.all_to_all(message, 'narrow', split_axis=0, concat_axis=0, tiled=True)]
    gather x5 -> x0, local copies, waits for them, and re-layouts: 10.1 us -> none  [the longest x3 6.97 us: per_device(): boundary_sites[arrived_node] - arrived_temp]
    scatter-add x2 -> x0, other arithmetic: 9.58 us -> none  [the longest x1 7.62 us: per_device(): jax.ops.segment_sum(interface_exchange * arrived_temp, arrived_node, num_...]
    all_to_all x3 -> x1, starting transfers between devices: 15.5 us -> 6.63 us  [per_device(): lax.all_to_all(message, 'narrow', split_axis=0, concat_axis=0, tiled=True)]
    pallas_call x0 -> x5, Pallas kernels: none -> 8.8 us  [call(): pl.pallas_call(kernel, out_shape=list(shapes), in_specs=specs, out_specs=...]
    unnamed x40 -> x0, other arithmetic: 4.27 us -> none
    scatter x2 -> x0, local copies, waits for them, and re-layouts: 2.97 us -> none  [the longest x1 1.56 us: per_device(): send_node = jnp.zeros((peer_count * capacity,), jnp.int32).at[slot_index]...]
    all_to_all x5 -> x0, local copies, waits for them, and re-layouts: 2.47 us -> none  [the longest x2 1.2 us: per_device(): lax.all_to_all(send_node, 'narrow', split_axis=0, concat_axis=0, tiled=True)]
  transfers between devices with their start and end apart: 7 -> 7, of which waited for: 5 -> 4; matrix products, arithmetic and copies ran while one was open for 4% -> 0% of each run, Pallas kernels for 0% -> 3%
where the time goes in v1:
time: 61.2 us; the launch traced here: 60.7 us
  starting transfers between devices  31.9 us (52%)
  waiting for transfers between devices  14.4 us (24%)
  Pallas kernels  8.8 us (14%)
  local copies, waits for them, and re-layouts  4.28 us (7%)
  between operations  1.41 us (2%)
    ppermute x6, starting transfers between devices, send(): lax.ppermute(block, axis, [(i, (i + step) % count) for i in range(count)])  25.3 us
    pallas_call x5, Pallas kernels, call(): pl.pallas_call(kernel, out_shape=list(shapes), in_specs=specs, out_specs=...  8.8 us
    ppermute x6, waiting for transfers between devices, send(): lax.ppermute(block, axis, [(i, (i + step) % count) for i in range(count)])  7.34 us
    all_to_all x1, waiting for transfers between devices, per_device(): lax.all_to_all(message, 'narrow', split_axis=0, concat_axis=0, tiled=True)  7.01 us
    all_to_all x1, starting transfers between devices, per_device(): lax.all_to_all(message, 'narrow', split_axis=0, concat_axis=0, tiled=True)  6.63 us
    unnamed x24, local copies, waits for them, and re-layouts  4.28 us
  transfers between devices with their start and end apart: 7, of which 4 were waited for; matrix products, arithmetic and copies ran while one was open for 0% of the time, Pallas kernels for 3%

profile of v1, /device:TPU:49, one launch (start us, length us, event | category | flops | bytes accessed | tf_op | source)
XLA Modules:
  0.0 60.7 jit_solution(5927189161650871336)
XLA Ops:
  0.6 0.0 copy-start
  0.7 1.1 %copy-done.1 = f32[19,8,8,128]{3,2,1,0:T(8,128)S(1)} copy-done((f32[19,8,8,128]{3,2,1,0:T(8,128)S(1)}, f32[19,8,8,128]{3,2,1,0:T(8,128)}, u32[]{:S(2)}) %copy-start.1) | copy-done | bytes 622616
  1.8 0.9 %copy-done.2 = f32[7,8,8,128]{3,2,1,0:T(8,128)S(1)} copy-done((f32[7,8,8,128]{3,2,1,0:T(8,128)S(1)}, f32[7,8,8,128]{3,2,1,0:T(8,128)}, u32[]{:S(2)}) %copy-start.2) | copy-done | bytes 229400
  2.7 0.8 %copy-done.3 = s32[8,8,128]{2,1,0:T(8,128)S(1)} copy-done((s32[8,8,128]{2,1,0:T(8,128)S(1)}, s32[8,8,128]{2,1,0:T(8,128)}, u32[]{:S(2)}) %copy-start.3) | copy-done | bytes 32792
  3.5 0.8 %copy-done.4 = f32[8,8,128]{2,1,0:T(8,128)S(1)} copy-done((f32[8,8,128]{2,1,0:T(8,128)S(1)}, f32[8,8,128]{2,1,0:T(8,128)}, u32[]{:S(2)}) %copy-start.4) | copy-done | bytes 32792
  4.2 0.3 shard_map.148
  4.6 0.0 copy-start.8
  4.6 4.9 %collective-permute-start = (f32[6,8,128]{2,1,0:T(8,128)S(1)}, f32[6,8,128]{2,1,0:T(8,128)S(1)}, u32[]{:S(2)}, u32[]{:S(2)}) collective-permute-start(f32[6,8,128]{2,1,0:T(8,128)S(1)} %get-tuple-element.21), channel_id=1, source_target_pairs={{0,16},{16,32},{32,48},{48,64},{64,80},{80,96},{96,112},{112,128},... | collective-permute-start | bytes 73736 | tf_op jit(solution)/shard_map/ppermute | solution.py:427
  9.5 16.4 %collective-permute-start.1 = (f32[6,8,128]{2,1,0:T(8,128)S(1)}, f32[6,8,128]{2,1,0:T(8,128)S(1)}, u32[]{:S(2)}, u32[]{:S(2)}) collective-permute-start(f32[6,8,128]{2,1,0:T(8,128)S(1)} %get-tuple-element.22), channel_id=1, source_target_pairs={{0,1008},{16,0},{32,16},{48,32},{64,48},{80,64},{96,80},{112,96},{... | collective-permute-start | bytes 73736 | tf_op jit(solution)/shard_map/ppermute | solution.py:427
  25.9 3.5 %collective-permute-start.2 = (f32[4,8,128]{2,1,0:T(8,128)S(1)}, f32[4,8,128]{2,1,0:T(8,128)S(1)}, u32[]{:S(2)}, u32[]{:S(2)}) collective-permute-start(f32[4,8,128]{2,1,0:T(8,128)S(1)} %get-tuple-element.23), channel_id=1, source_target_pairs={{0,1},{1,2},{2,3},{3,4},{4,5},{5,6},{6,7},{7,8},{8,9},{9,10},{10,1... | collective-permute-start | bytes 49160 | tf_op jit(solution)/shard_map/ppermute | solution.py:427
  30.1 0.9 %shard_map.149 = (f32[16,256]{1,0:T(8,128)S(1)}, f32[16,256]{1,0:T(8,128)S(1)}) custom-call(f32[1,16,256]{2,1,0:T(8,128)S(1)} %copy-done.5, f32[1]{0:T(128)S(6)} %copy.16.uptake_ref, f32[16,16]{1,0:T(8,128)S(1)} %copy-done.8, f32[256,256]{1,0:T(8,128)S(1)} %copy-done, f32[16,256]{1,0:T(8,128)S(1)} %copy-done.7, f32[16,256]{1,0:T(8,128)S(1)} %copy-done.6), custom_call_target="tpu_custom_call" | custom-call | flops 1000000 | bytes 345092 | tf_op jit(solution)/shard_map/pallas_call | solution.py:373
  30.9 2.8 %collective-permute-done.3.yd_ref = f32[4,8,128]{2,1,0:T(8,128)S(1)} collective-permute-done((f32[4,8,128]{2,1,0:T(8,128)S(1)}, f32[4,8,128]{2,1,0:T(8,128)S(1)}, u32[]{:S(2)}, u32[]{:S(2)}) %collective-permute-start.3) | collective-permute-done | bytes 16416 | tf_op jit(solution)/shard_map/ppermute | solution.py:427
  33.8 0.7 %copy-done.10 = s32[256,1]{0,1:T(1,128)S(1)} copy-done((s32[256,1]{0,1:T(1,128)S(1)}, s32[256,1]{0,1:T(1,128)}, u32[]{:S(2)}) %copy-start.10) | copy-done | bytes 1048
  34.4 0.0 copy-done.11
  34.4 0.0 copy-done.9
  34.4 1.0 %shard_map.150 = (f32[7,8,8,128]{3,2,1,0:T(8,128)S(1)}, f32[1,256]{1,0:T(1,128)S(1)}, f32[64,8,128]{2,1,0:T(8,128)}, f32[2,8,128]{2,1,0:T(8,128)S(1)}, f32[2,8,128]{2,1,0:T(8,128)S(1)}) custom-call(f32[7,8,8,128]{3,2,1,0:T(8,128)S(1)} %get-tuple-element.25.heat_post_ref, f32[6,8,128]{2,1,0:T(8,128)S(1)} %collective-permute-done.xu_ref, ...), custom_call_target="tpu_custom_call" | custom-call | flops 1000000 | bytes 872452 | tf_op jit(solution)/shard_map/pallas_call | solution.py:373
  35.4 6.6 %all-to-all-start = ((f32[64,8,128]{2,1,0:T(8,128)}), f32[64,8,128]{2,1,0:T(8,128)S(1)}, u32[]{:S(2)}, u32[]{:S(2)}) async-start(f32[64,8,128]{2,1,0:T(8,128)} %get-tuple-element.32), calls=%async_computation | async-start | bytes 524288 | tf_op jit(solution)/shard_map/all_to_all | solution.py:440
  42.0 0.5 collective-permute-start.4
  42.5 0.0 collective-permute-start.5
  42.6 0.8 %collective-permute-done.4.du_ref = f32[2,8,128]{2,1,0:T(8,128)S(1)} collective-permute-done((f32[2,8,128]{2,1,0:T(8,128)S(1)}, f32[2,8,128]{2,1,0:T(8,128)S(1)}, u32[]{:S(2)}, u32[]{:S(2)}) %collective-permute-start.4) | collective-permute-done | bytes 8224 | tf_op jit(solution)/shard_map/ppermute | solution.py:427
  43.3 3.8 %collective-permute-done.5.dd_ref = f32[2,8,128]{2,1,0:T(8,128)S(1)} collective-permute-done((f32[2,8,128]{2,1,0:T(8,128)S(1)}, f32[2,8,128]{2,1,0:T(8,128)S(1)}, u32[]{:S(2)}, u32[]{:S(2)}) %collective-permute-start.5) | collective-permute-done | bytes 8224 | tf_op jit(solution)/shard_map/ppermute | solution.py:427
  47.1 1.0 %shard_map.151 = f32[19,8,8,128]{3,2,1,0:T(8,128)} custom-call(f32[19,8,8,128]{3,2,1,0:T(8,128)S(1)} %get-tuple-element.20.post_ref, f32[6,8,128]{2,1,0:T(8,128)S(1)} %collective-permute-done.xu_ref, f32[6,8,128]{2,1,0:T(8,128)S(1)} %collective-permute-done.1.xd_ref, f32[4,8,128]{2,1,0:T(8,128)S(1)} %collective-permute-done.2.yu_ref, ...), custom_call_target="tpu_custom_call" | custom-call | flops 1000000 | bytes 1343488 | tf_op jit(solution)/shard_map/pallas_call | solution.py:373
  48.1 7.0 %all-to-all-done = f32[64,8,128]{2,1,0:T(8,128)S(1)} async-done(((f32[64,8,128]{2,1,0:T(8,128)}), f32[64,8,128]{2,1,0:T(8,128)S(1)}, u32[]{:S(2)}, u32[]{:S(2)}) %all-to-all-start) | async-done | bytes 262176 | tf_op jit(solution)/shard_map/all_to_all | solution.py:440
  55.1 5.6 %shard_map.152 = (f32[7,8,8,128]{3,2,1,0:T(8,128)}, f32[1,16,256]{2,1,0:T(8,128)}) custom-call(f32[512,128]{1,0:T(8,128)S(1)} %bitcast.6, f32[7,8,8,128]{3,2,1,0:T(8,128)S(1)} %get-tuple-element.33.passed_ref, f32[1,256]{1,0:T(1,128)S(1)} %get-tuple-element.34.warmth_ref, s32[2,128]{1,0:T(2,128)S(1)} %bitcast.8, s32[2,128]{1,0:T(2,128)S(1)} %bitcast.10, ...), custom_call_target="tpu_custom_call" | custom-call | flops 1000000 | bytes 1036292 | tf_op jit(solution)/shard_map/pallas_call | solution.py:373
  (19 shorter events, 0.0 us)
Async XLA Ops:
  0.6 29.4 %copy-start = (f32[256,256]{1,0:T(8,128)S(1)}, f32[256,256]{1,0:T(8,128)}, u32[]{:S(2)}) copy-start(f32[256,256]{1,0:T(8,128)} %constant.18.clone.plane_ref) | copy-start | bytes 786436
  0.6 1.1 %copy-start.1 = (f32[19,8,8,128]{3,2,1,0:T(8,128)S(1)}, f32[19,8,8,128]{3,2,1,0:T(8,128)}, u32[]{:S(2)}) copy-start(f32[19,8,8,128]{3,2,1,0:T(8,128)} %flow_ref.1) | copy-start | bytes 1867780
  1.8 0.9 %copy-start.2 = (f32[7,8,8,128]{3,2,1,0:T(8,128)S(1)}, f32[7,8,8,128]{3,2,1,0:T(8,128)}, u32[]{:S(2)}) copy-start(f32[7,8,8,128]{3,2,1,0:T(8,128)} %heat_ref.1) | copy-start | bytes 688132
  2.7 0.8 %copy-start.3 = (s32[8,8,128]{2,1,0:T(8,128)S(1)}, s32[8,8,128]{2,1,0:T(8,128)}, u32[]{:S(2)}) copy-start(s32[8,8,128]{2,1,0:T(8,128)} %mask_ref.1) | copy-start | bytes 98308
  3.5 0.8 %copy-start.4 = (f32[8,8,128]{2,1,0:T(8,128)S(1)}, f32[8,8,128]{2,1,0:T(8,128)}, u32[]{:S(2)}) copy-start(f32[8,8,128]{2,1,0:T(8,128)} %rate_ref.1) | copy-start | bytes 98308
  4.2 25.8 %copy-start.5 = (f32[1,16,256]{2,1,0:T(8,128)S(1)}, f32[1,16,256]{2,1,0:T(8,128)}, u32[]{:S(2)}) copy-start(f32[1,16,256]{2,1,0:T(8,128)} %source_ref.1) | copy-start | bytes 49156
  4.2 25.8 %copy-start.6 = (f32[16,256]{1,0:T(8,128)S(1)}, f32[16,256]{1,0:T(8,128)}, u32[]{:S(2)}) copy-start(f32[16,256]{1,0:T(8,128)} %constant.20.clone.first_ref) | copy-start | bytes 49156
  4.2 25.8 %copy-start.7 = (f32[16,256]{1,0:T(8,128)S(1)}, f32[16,256]{1,0:T(8,128)}, u32[]{:S(2)}) copy-start(f32[16,256]{1,0:T(8,128)} %constant.19.clone.total_ref) | copy-start | bytes 49156
  4.6 25.5 %copy-start.8 = (f32[16,16]{1,0:T(8,128)S(1)}, f32[16,16]{1,0:T(8,128)}, u32[]{:S(2)}) copy-start(f32[16,16]{1,0:T(8,128)} %constant.17.clone.sine_ref) | copy-start | bytes 3076
  4.6 29.1 %collective-permute-start = (f32[6,8,128]{2,1,0:T(8,128)S(1)}, f32[6,8,128]{2,1,0:T(8,128)S(1)}, u32[]{:S(2)}, u32[]{:S(2)}) collective-permute-start(f32[6,8,128]{2,1,0:T(8,128)S(1)} %get-tuple-element.21), channel_id=1, source_target_pairs={{0,16},{16,32},{32,48},{48,64},{64,80},{80,96},{96,112},{112,128},... | collective-permute-start | bytes 73736 | tf_op jit(solution)/shard_map/ppermute | solution.py:427
  9.5 24.2 %collective-permute-start.1 = (f32[6,8,128]{2,1,0:T(8,128)S(1)}, f32[6,8,128]{2,1,0:T(8,128)S(1)}, u32[]{:S(2)}, u32[]{:S(2)}) collective-permute-start(f32[6,8,128]{2,1,0:T(8,128)S(1)} %get-tuple-element.22), channel_id=1, source_target_pairs={{0,1008},{16,0},{32,16},{48,32},{64,48},{80,64},{96,80},{112,96},{... | collective-permute-start | bytes 73736 | tf_op jit(solution)/shard_map/ppermute | solution.py:427
  25.9 5.1 %collective-permute-start.2 = (f32[4,8,128]{2,1,0:T(8,128)S(1)}, f32[4,8,128]{2,1,0:T(8,128)S(1)}, u32[]{:S(2)}, u32[]{:S(2)}) collective-permute-start(f32[4,8,128]{2,1,0:T(8,128)S(1)} %get-tuple-element.23), channel_id=1, source_target_pairs={{0,1},{1,2},{2,3},{3,4},{4,5},{5,6},{6,7},{7,8},{8,9},{9,10},{10,1... | collective-permute-start | bytes 49160 | tf_op jit(solution)/shard_map/ppermute | solution.py:427
  29.3 4.4 %collective-permute-start.3 = (f32[4,8,128]{2,1,0:T(8,128)S(1)}, f32[4,8,128]{2,1,0:T(8,128)S(1)}, u32[]{:S(2)}, u32[]{:S(2)}) collective-permute-start(f32[4,8,128]{2,1,0:T(8,128)S(1)} %get-tuple-element.24), channel_id=1, source_target_pairs={{0,15},{1,0},{2,1},{3,2},{4,3},{5,4},{6,5},{7,6},{8,7},{9,8},{10,9... | collective-permute-start | bytes 49160 | tf_op jit(solution)/shard_map/ppermute | solution.py:427
  33.7 0.7 %copy-start.10 = (s32[256,1]{0,1:T(1,128)S(1)}, s32[256,1]{0,1:T(1,128)}, u32[]{:S(2)}) copy-start(s32[256,1]{0,1:T(1,128)} %param.19) | copy-start | bytes 3076
  33.7 0.7 %copy-start.11 = (s32[256]{0:T(256)S(1)}, s32[256]{0:T(256)}, u32[]{:S(2)}) copy-start(s32[256]{0:T(256)} %param.21) | copy-start | bytes 3076
  33.7 0.7 %copy-start.9 = (s32[256]{0:T(256)S(1)}, s32[256]{0:T(256)}, u32[]{:S(2)}) copy-start(s32[256]{0:T(256)} %param.20) | copy-start | bytes 3076
  35.4 19.7 %all-to-all-start = ((f32[64,8,128]{2,1,0:T(8,128)}), f32[64,8,128]{2,1,0:T(8,128)S(1)}, u32[]{:S(2)}, u32[]{:S(2)}) async-start(f32[64,8,128]{2,1,0:T(8,128)} %get-tuple-element.32), calls=%async_computation | async-start | bytes 524288 | tf_op jit(solution)/shard_map/all_to_all | solution.py:440
  42.0 1.3 %collective-permute-start.4 = (f32[2,8,128]{2,1,0:T(8,128)S(1)}, f32[2,8,128]{2,1,0:T(8,128)S(1)}, u32[]{:S(2)}, u32[]{:S(2)}) collective-permute-start(f32[2,8,128]{2,1,0:T(8,128)S(1)} %get-tuple-element.30), channel_id=1, source_target_pairs={{0,1},{1,2},{2,3},{3,4},{4,5},{5,6},{6,7},{7,8},{8,9},{9,10},{10,1... | collective-permute-start | bytes 24584 | tf_op jit(solution)/shard_map/ppermute | solution.py:427
  42.5 4.6 %collective-permute-start.5 = (f32[2,8,128]{2,1,0:T(8,128)S(1)}, f32[2,8,128]{2,1,0:T(8,128)S(1)}, u32[]{:S(2)}, u32[]{:S(2)}) collective-permute-start(f32[2,8,128]{2,1,0:T(8,128)S(1)} %get-tuple-element.31), channel_id=1, source_target_pairs={{0,15},{1,0},{2,1},{3,2},{4,3},{5,4},{6,5},{7,6},{8,7},{9,8},{10,9... | collective-permute-start | bytes 24584 | tf_op jit(solution)/shard_map/ppermute | solution.py:427

commit v2 on v1

--- a/solution.py
+++ b/solution.py
@@ -41,13 +41,11 @@
 
 x_up = (1, 7, 9, 11, 13)
 x_down = (2, 8, 10, 12, 14)
-y_up = (3, 15, 17)
-y_down = (4, 16, 18)
-diagonal_up = (7, 10)
-diagonal_down = (8, 9)
+y_up = (3, 15, 17, 7, 10)
+y_down = (4, 16, 18, 8, 9)
 
 HIGHEST = lax.Precision.HIGHEST
-params = pltpu.CompilerParams(vmem_limit_bytes=32 * 1024 * 1024)
+limit = 32 * 1024 * 1024
 
 
 def sine_constants(size):
@@ -90,9 +88,13 @@
     return jnp.where(numbers == row, 1.0, 0.0).astype(jnp.bfloat16)
 
 
+def first_kernel(me_ref, out_ref):
+    out_ref[...] = jnp.full(out_ref.shape, me_ref[0], jnp.int32)
+
+
 def collide_kernel(
-    flow_ref, heat_ref, mask_ref, rate_ref,
-    post_ref, heat_post_ref, xu_ref, xd_ref, yu_ref, yd_ref, du_ref, dd_ref,
+    flow_ref, heat_ref, mask_ref, rate_ref, _,
+    post_ref, heat_post_ref, xu_ref, xd_ref, yu_ref, yd_ref,
 ):
     wide_x, wide_y = flow_ref.shape[1], flow_ref.shape[2]
     for x in range(wide_x):
@@ -159,20 +161,60 @@
             yu_ref[slot, row, :] = part[last]
         for slot, part in enumerate([heat[4]] + [post[i] for i in y_down]):
             yd_ref[slot, row, :] = part[0:1]
-        for slot, i in enumerate(diagonal_up):
-            du_ref[slot, row, :] = post[i][last]
-        for slot, i in enumerate(diagonal_down):
-            dd_ref[slot, row, :] = post[i][0:1]
 
 
 def block_kernel(
-    source_ref, uptake_ref, sine_ref, plane_ref, total_ref, first_ref, cube_ref, reply_ref
+    source_ref, site_ref, owner_ref, node_ref, uptake_ref, wide_ref,
+    sine_ref, plane_ref, total_ref, first_ref,
+    cube_ref, reply_ref, part_ref, at_plane_ref, at_depth_ref, at_owner_ref, at_node_ref,
+    *, n_wide, face, depth,
 ):
     sine, plane = sine_ref[...], plane_ref[...]
     inverse = 1.0 / (total_ref[...] + uptake_ref[0])
     spectral = dot(dot(sine, source_ref[0], HIGHEST), plane, HIGHEST) * inverse
-    cube_ref[...] = dot(dot(sine, spectral, HIGHEST), plane, HIGHEST)
-    reply_ref[...] = dot(sine, first_ref[...] * inverse, HIGHEST)
+    cube = dot(dot(sine, spectral, HIGHEST), plane, HIGHEST)
+    reply = dot(sine, first_ref[...] * inverse, HIGHEST)
+    cube_ref[...] = cube
+    reply_ref[...] = reply
+    owners, nodes, sites = owner_ref[...], node_ref[...], site_ref[...]
+    number = ((owners * n_wide + wide_ref[0]) * face + nodes).astype(jnp.float32)
+    half = face // 2
+    part_ref[...] = jnp.concatenate(
+        [
+            number, cube[0:1, 0:half], cube[0:1, half:], reply[0:1, 0:half], reply[0:1, half:],
+            number,
+        ],
+        axis=0,
+    )
+    flat = lambda rows: jnp.concatenate([rows[0:1], rows[1:2]], axis=1)
+    at_plane_ref[...] = one_hot(flat(sites // depth), at_plane_ref.shape[0])
+    at_depth_ref[...] = one_hot(flat(sites % depth), at_depth_ref.shape[0])
+    at_owner_ref[...] = one_hot(flat(owners), at_owner_ref.shape[0])
+    at_node_ref[...] = one_hot(flat(nodes), at_node_ref.shape[0])
+
+
+def moved_x(rows, direction, edge):
+    size = rows.shape[0]
+    numbers = lax.broadcasted_iota(jnp.int32, rows.shape, 0)
+    if direction > 0:
+        return jnp.where(numbers == 0, edge, pltpu.roll(rows, 1, 0))
+    return jnp.where(numbers == size - 1, edge, pltpu.roll(rows, size - 1, 0))
+
+
+def rim_kernel(yu_raw_ref, yd_raw_ref, xu_ref, xd_ref, yu_ref, yd_ref):
+    last = xu_ref.shape[1] - 1
+    for raw_ref, out_ref, names, y in (
+        (yu_raw_ref, yu_ref, y_up, last),
+        (yd_raw_ref, yd_ref, y_down, 0),
+    ):
+        out_ref[0] = raw_ref[0]
+        for slot, i in enumerate(names, 1):
+            direction = int(flow_velocity[i, 0])
+            rows = raw_ref[slot]
+            if direction:
+                edges, at = (xu_ref, x_up) if direction > 0 else (xd_ref, x_down)
+                rows = moved_x(rows, direction, edges[1 + at.index(i), y : y + 1, :])
+            out_ref[slot] = rows
 
 
 def shifted_y(value, direction, edge):
@@ -189,16 +231,9 @@
     return pltpu.roll(value, 1 if direction > 0 else value.shape[1] - 1, 1)
 
 
-def site_one_hots(site_ref, planes, depth):
-    rows = site_ref[...]
-    row = jnp.concatenate([rows[0:1], rows[1:2]], axis=1)
-    return one_hot(row // depth, planes), one_hot(row % depth, depth)
-
-
 def warmth_kernel(
-    heat_post_ref, xu_ref, xd_ref, yu_ref, yd_ref, du_ref, dd_ref,
-    site_ref, owner_ref, node_ref, wide_ref, cube_ref, reply_ref,
-    passed_ref, warmth_ref, send_ref, du_out_ref, dd_out_ref, *, n_wide, face,
+    heat_post_ref, xu_ref, xd_ref, yu_ref, yd_ref, part_ref, at_plane_ref, at_depth_ref,
+    passed_ref, warmth_ref, send_ref,
 ):
     wide_x, wide_y, depth = heat_post_ref.shape[1:]
     planes = []
@@ -217,46 +252,17 @@
         planes.append(functools.reduce(lambda a, b: a + b, passed))
     field = jnp.concatenate(planes, axis=0)
     count = wide_x * wide_y
-    at_plane, at_depth = site_one_hots(site_ref, count, depth)
-    picked = dot(jnp.concatenate(parts_of(field, 3), axis=0), at_depth)
+    picked = dot(jnp.concatenate(parts_of(field, 3), axis=0), at_depth_ref[...])
     picked = picked[0:count] + picked[count : 2 * count] + picked[2 * count :]
-    warmth = jnp.sum(picked * at_plane.astype(jnp.float32), axis=0, keepdims=True)
+    warmth = jnp.sum(picked * at_plane_ref[...].astype(jnp.float32), axis=0, keepdims=True)
     warmth_ref[...] = warmth
-    number = ((owner_ref[...] * n_wide + wide_ref[0]) * face + node_ref[...]).astype(jnp.float32)
-    half = face // 2
-    message = jnp.concatenate(
-        [
-            warmth[:, 0:half], warmth[:, half:], number,
-            cube_ref[0:1, 0:half], cube_ref[0:1, half:],
-            reply_ref[0:1, 0:half], reply_ref[0:1, half:],
-        ],
-        axis=0,
-    )
+    half = warmth.shape[1] // 2
+    message = jnp.concatenate([warmth[:, 0:half], warmth[:, half:], part_ref[0:6]], axis=0)
     for peer in range(send_ref.shape[0]):
         send_ref[peer] = message
-    for slot, i in enumerate(diagonal_up):
-        rows = lax.broadcasted_iota(jnp.int32, (wide_x, depth), 0)
-        if flow_velocity[i, 0] > 0:
-            edge = xu_ref[1 + x_up.index(i), wide_y - 1 : wide_y, :]
-            du_out_ref[slot] = jnp.where(rows == 0, edge, pltpu.roll(du_ref[slot], 1, 0))
-        else:
-            edge = xd_ref[1 + x_down.index(i), wide_y - 1 : wide_y, :]
-            du_out_ref[slot] = jnp.where(
-                rows == wide_x - 1, edge, pltpu.roll(du_ref[slot], wide_x - 1, 0)
-            )
-    for slot, i in enumerate(diagonal_down):
-        rows = lax.broadcasted_iota(jnp.int32, (wide_x, depth), 0)
-        if flow_velocity[i, 0] > 0:
-            edge = xu_ref[1 + x_up.index(i), 0:1, :]
-            dd_out_ref[slot] = jnp.where(rows == 0, edge, pltpu.roll(dd_ref[slot], 1, 0))
-        else:
-            edge = xd_ref[1 + x_down.index(i), 0:1, :]
-            dd_out_ref[slot] = jnp.where(
-                rows == wide_x - 1, edge, pltpu.roll(dd_ref[slot], wide_x - 1, 0)
-            )
-
-
-def stream_kernel(post_ref, xu_ref, xd_ref, yu_ref, yd_ref, du_ref, dd_ref, out_ref):
+
+
+def stream_kernel(post_ref, xu_ref, xd_ref, yu_ref, yd_ref, out_ref):
     wide_x = post_ref.shape[1]
     for i in range(19):
         cx, cy, cz = (int(c) for c in flow_velocity[i])
@@ -268,20 +274,16 @@
             else:
                 value = post_ref[i, x - cx]
             if cy:
-                if cx:
-                    edges = du_ref if cy > 0 else dd_ref
-                    slot = (diagonal_up if cy > 0 else diagonal_down).index(i)
-                else:
-                    edges = yu_ref if cy > 0 else yd_ref
-                    slot = 1 + (y_up if cy > 0 else y_down).index(i)
-                value = shifted_y(value, cy, edges[slot, x : x + 1, :])
+                edges, at = (yu_ref, y_up) if cy > 0 else (yd_ref, y_down)
+                value = shifted_y(value, cy, edges[1 + at.index(i), x : x + 1, :])
             out_ref[i, x] = shifted_z(value, cz)
 
 
 def finish_kernel(
-    got_ref, passed_ref, warmth_ref, site_ref, owner_ref, node_ref, me_ref, cube_ref, reply_ref,
-    plane_ref, heat_ref, cube_out_ref, high_ref, low_ref, owner_rows_ref, node_rows_ref, table_ref,
-    *, n_wide, face,
+    got_ref, passed_ref, warmth_ref, at_plane_ref, at_depth_ref, at_owner_ref, at_node_ref,
+    me_ref, cube_ref, reply_ref, plane_ref,
+    heat_ref, cube_out_ref,
+    high_ref, low_ref, owner_rows_ref, node_columns_ref, table_ref, *, n_wide, face,
 ):
     peers, depth = got_ref.shape[0] // 8, got_ref.shape[1]
     wide_x, wide_y = passed_ref.shape[1:3]
@@ -293,29 +295,27 @@
         low_ref[half] = temperature - high
         number = bits(2 + half).astype(jnp.int32)
         owner_rows_ref[half] = (number // (n_wide * face)).astype(jnp.float32)
-        node_rows_ref[half] = (number % face).astype(jnp.float32)
+        node_columns_ref[half] = (number % face).astype(jnp.float32).T
 
     def spread(ref, half, d):
-        row = ref[half, pl.ds(d, 1), :]
+        row = ref[half, d : d + 1, :]
         return jnp.broadcast_to(row, (16, depth)).astype(jnp.bfloat16)
 
     numbers = lax.broadcasted_iota(jnp.int32, (16, depth), 0).astype(jnp.float32)
-    zero = jnp.zeros((16, depth), jnp.bfloat16)
-    one = jnp.ones((16, depth), jnp.bfloat16)
+    lanes = lax.broadcasted_iota(jnp.int32, (depth, face), 1).astype(jnp.float32)
+    lanes = lanes.astype(jnp.bfloat16)
+    zero, one = jnp.bfloat16(0), jnp.bfloat16(1)
     owner_groups = -(-peers // 16)
-
-    def step(block, total):
+    wanted = [(numbers + 16.0 * g).astype(jnp.bfloat16) for g in range(owner_groups)]
+    both = jnp.zeros((2 * 16 * owner_groups, face), jnp.float32)
+    chunk = math.gcd(peers, 8)
+    for start in range(0, peers, chunk):
         left, right = [], []
-        for inner in range(unroll):
-            d = block * unroll + inner
+        for d in range(start, start + chunk):
             for half in range(2):
-                node, owner = spread(node_rows_ref, half, d), spread(owner_rows_ref, half, d)
+                owner = spread(owner_rows_ref, half, d)
                 high, low = spread(high_ref, half, d), spread(low_ref, half, d)
-                wanted = [(numbers + 16.0 * g).astype(jnp.bfloat16) for g in range(face // 16)]
-                right.append(
-                    jnp.concatenate([jnp.where(node == w, one, zero) for w in wanted], axis=0)
-                )
-                hits = [owner == wanted[g] for g in range(owner_groups)]
+                hits = [owner == w for w in wanted]
                 left.append(
                     jnp.concatenate(
                         [jnp.where(hit, high, zero) for hit in hits]
@@ -323,14 +323,10 @@
                         axis=0,
                     )
                 )
-        return total + dot_last(
-            jnp.concatenate(left, axis=1), jnp.concatenate(right, axis=1)
-        )
-
-    unroll = math.gcd(peers, 8)
-    both = lax.fori_loop(
-        0, peers // unroll, step, jnp.zeros((2 * 16 * owner_groups, face), jnp.float32)
-    )
+                node = node_columns_ref[half, :, d : d + 1].astype(jnp.bfloat16)
+                hit = jnp.broadcast_to(node, (depth, face)) == lanes
+                right.append(jnp.where(hit, one, zero))
+        both = both + dot(jnp.concatenate(left, axis=1), jnp.concatenate(right, axis=0))
     table = interface_exchange * (both[0:peers] + both[16 * owner_groups :][0:peers])
     plane = plane_ref[...]
     spectral = dot(table, plane, HIGHEST)
@@ -343,19 +339,16 @@
     surface = answers[0:peers] + jnp.concatenate([bits(4), bits(5)], axis=1)
     cube_out_ref[0] = cube_ref[...] + answers[peers:]
 
-    owners, nodes = owner_ref[...], node_ref[...]
-    at_owner = one_hot(jnp.concatenate([owners[0:1], owners[1:2]], axis=1), peers)
-    at_node = one_hot(jnp.concatenate([nodes[0:1], nodes[1:2]], axis=1), face)
-    picked = dot(jnp.concatenate(parts_of(surface, 3), axis=0), at_node)
+    picked = dot(jnp.concatenate(parts_of(surface, 3), axis=0), at_node_ref[...])
     picked = picked[0:peers] + picked[peers : 2 * peers] + picked[2 * peers :]
-    boundary = jnp.sum(picked * at_owner.astype(jnp.float32), axis=0, keepdims=True)
+    boundary = jnp.sum(picked * at_owner_ref[...].astype(jnp.float32), axis=0, keepdims=True)
     flux = interface_exchange * (boundary - warmth_ref[...])
     count = wide_x * wide_y
-    at_plane, at_depth = site_one_hots(site_ref, count, depth)
+    at_plane = at_plane_ref[...]
     flux_parts = [
         at_plane * jnp.broadcast_to(part, at_plane.shape) for part in parts_of(flux, 3)
     ]
-    gain = dot_last(jnp.concatenate(flux_parts, axis=0), at_depth)
+    gain = dot_last(jnp.concatenate(flux_parts, axis=0), at_depth_ref[...])
     gain = gain[0:count] + gain[count : 2 * count] + gain[2 * count :]
     for x in range(wide_x):
         rows = gain[x * wide_y : (x + 1) * wide_y]
@@ -364,25 +357,25 @@
 
 
 def call(kernel, shapes, *operands, smem=(), scratch=(), cost=1000000):
-    specs = [
-        pl.BlockSpec(memory_space=pltpu.SMEM if i in smem else pltpu.VMEM)
-        for i in range(len(operands))
-    ]
-    out_specs = [pl.BlockSpec(memory_space=pltpu.VMEM) for _ in shapes]
+    spaces = [pltpu.SMEM if i in smem else pltpu.VMEM for i in range(len(operands))]
     moved = sum(4 * math.prod(o.shape) for o in list(operands) + list(shapes))
     return pl.pallas_call(
         kernel,
         out_shape=list(shapes),
-        in_specs=specs,
-        out_specs=out_specs,
+        in_specs=[pl.BlockSpec(memory_space=space) for space in spaces],
+        out_specs=[pl.BlockSpec(memory_space=pltpu.VMEM) for _ in shapes],
         scratch_shapes=list(scratch),
-        compiler_params=params,
+        compiler_params=pltpu.CompilerParams(vmem_limit_bytes=limit),
         cost_estimate=pl.CostEstimate(flops=cost, bytes_accessed=moved, transcendentals=0),
     )(*operands)
 
 
 def f32(*shape):
     return jax.ShapeDtypeStruct(shape, jnp.float32)
+
+
+def b16(*shape):
+    return jax.ShapeDtypeStruct(shape, jnp.bfloat16)
 
 
 def per_device(
@@ -407,19 +400,26 @@
     wide = lax.axis_index("wide").astype(jnp.int32).reshape(1)
     sine, plane, total, first = (jnp.asarray(c) for c in sine_constants(size))
 
-    post, heat_post, xu, xd, yu, yd, du, dd = call(
+    (early,) = call(
+        first_kernel, (jax.ShapeDtypeStruct((8, nz), jnp.int32),), me, smem=(0,), cost=10**10
+    )
+    post, heat_post, xu, xd, yu, yd = call(
         collide_kernel,
         (
             f32(19, bx, by, nz), f32(7, bx, by, nz), f32(6, by, nz), f32(6, by, nz),
-            f32(4, bx, nz), f32(4, bx, nz), f32(2, bx, nz), f32(2, bx, nz),
+            f32(6, bx, nz), f32(6, bx, nz),
         ),
-        flow_state, thermal_distributions_current, fluid_mask, heat_rate,
-    )
-    cube, reply = call(
-        block_kernel,
-        (f32(size, face), f32(size, face)),
-        solid_source, cube_uptake_coefficients, sine, plane, total, first,
-        smem=(1,),
+        flow_state, thermal_distributions_current, fluid_mask, heat_rate, early,
+    )
+    cube, reply, part, at_plane, at_depth, at_owner, at_node = call(
+        functools.partial(block_kernel, n_wide=n_wide, face=face, depth=nz),
+        (
+            f32(size, face), f32(size, face), f32(8, face // 2),
+            b16(bx * by, rows), b16(nz, rows), b16(peers, rows), b16(face, rows),
+        ),
+        solid_source, site, owner, node, cube_uptake_coefficients, wide,
+        sine, plane, total, first,
+        smem=(4, 5),
     )
 
     def send(block, axis, step):
@@ -427,29 +427,23 @@
         return lax.ppermute(block, axis, [(i, (i + step) % count) for i in range(count)])
 
     xu, xd = send(xu, "narrow", 1), send(xd, "narrow", -1)
+    yu, yd = call(rim_kernel, (f32(6, bx, nz), f32(6, bx, nz)), yu, yd, xu, xd)
     yu, yd = send(yu, "wide", 1), send(yd, "wide", -1)
-    passed, warmth, message, du, dd = call(
-        functools.partial(warmth_kernel, n_wide=n_wide, face=face),
-        (
-            f32(7, bx, by, nz), f32(1, rows), f32(peers, 8, face // 2),
-            f32(2, bx, nz), f32(2, bx, nz),
-        ),
-        heat_post, xu, xd, yu, yd, du, dd, site, owner, node, wide, cube, reply,
-        smem=(10,),
+    passed, warmth, message = call(
+        warmth_kernel,
+        (f32(7, bx, by, nz), f32(1, rows), f32(peers, 8, face // 2)),
+        heat_post, xu, xd, yu, yd, part, at_plane, at_depth,
     )
     got = lax.all_to_all(message, "narrow", split_axis=0, concat_axis=0, tiled=True)
-    du, dd = send(du, "wide", 1), send(dd, "wide", -1)
-    (stream,) = call(
-        stream_kernel, (f32(19, bx, by, nz),), post, xu, xd, yu, yd, du, dd
-    )
+    (stream,) = call(stream_kernel, (f32(19, bx, by, nz),), post, xu, xd, yu, yd)
     heat, cubes = call(
         functools.partial(finish_kernel, n_wide=n_wide, face=face),
         (f32(7, bx, by, nz), f32(1, size, face)),
-        got.reshape(peers * 8, face // 2), passed, warmth, site, owner, node, me, cube, reply,
-        plane,
-        smem=(6,),
-        scratch=[pltpu.VMEM((2, peers, face // 2), jnp.float32)] * 4
-        + [pltpu.VMEM((peers, face), jnp.float32)],
+        got.reshape(peers * 8, face // 2), passed, warmth, at_plane, at_depth, at_owner, at_node,
+        me, cube, reply, plane,
+        smem=(7,),
+        scratch=[pltpu.VMEM((2, peers, face // 2), jnp.float32)] * 3
+        + [pltpu.VMEM((2, face // 2, peers), jnp.float32), pltpu.VMEM((peers, face), jnp.float32)],
     )
     return stream, heat, cubes
 

time: 61.2 us -> 59.9 us (0.979)
  local copies, waits for them, and re-layouts: 4.28 us -> 1.72 us
  starting transfers between devices: 31.9 us -> 34.3 us
  Pallas kernels: 8.8 us -> 6.86 us
  waiting for transfers between devices: 14.4 us -> 15.3 us
    all_to_all x1, waiting for transfers between devices: 7.01 us -> 12.1 us  [per_device(): lax.all_to_all(message, 'narrow', split_axis=0, concat_axis=0, tiled=True)]
    ppermute x6 -> x4, waiting for transfers between devices: 7.34 us -> 3.14 us  [send(): lax.ppermute(block, axis, [(i, (i + step) % count) for i in range(count)])]
    unnamed x24, local copies, waits for them, and re-layouts: 4.28 us -> 1.72 us
    all_to_all x1, starting transfers between devices: 6.63 us -> 9.03 us  [per_device(): lax.all_to_all(message, 'narrow', split_axis=0, concat_axis=0, tiled=True)]
    pallas_call x5 -> x7, Pallas kernels: 8.8 us -> 6.86 us  [call(): pl.pallas_call(kernel, out_shape=list(shapes), in_specs=[pl.BlockSpec(mem...]
    ppermute x6 -> x4, starting transfers between devices: 25.3 us -> 25.3 us  [send(): lax.ppermute(block, axis, [(i, (i + step) % count) for i in range(count)])]
  transfers between devices with their start and end apart: 7 -> 5, of which waited for: 4 -> 3; matrix products, arithmetic and copies ran while one was open for 0% -> 0% of each run, Pallas kernels for 3% -> 3%
where the time goes in v2:
time: 59.9 us; the launch traced here: 59.6 us
  starting transfers between devices  34.3 us (57%)
  waiting for transfers between devices  15.3 us (26%)
  Pallas kernels  6.86 us (11%)
  local copies, waits for them, and re-layouts  1.72 us (3%)
  between operations  1.47 us (2%)
    ppermute x4, starting transfers between devices, send(): lax.ppermute(block, axis, [(i, (i + step) % count) for i in range(count)])  25.3 us
    all_to_all x1, waiting for transfers between devices, per_device(): lax.all_to_all(message, 'narrow', split_axis=0, concat_axis=0, tiled=True)  12.1 us
    all_to_all x1, starting transfers between devices, per_device(): lax.all_to_all(message, 'narrow', split_axis=0, concat_axis=0, tiled=True)  9.03 us
    pallas_call x7, Pallas kernels, call(): pl.pallas_call(kernel, out_shape=list(shapes), in_specs=[pl.BlockSpec(mem...  6.86 us
    ppermute x4, waiting for transfers between devices, send(): lax.ppermute(block, axis, [(i, (i + step) % count) for i in range(count)])  3.14 us
    unnamed x24, local copies, waits for them, and re-layouts  1.72 us
  transfers between devices with their start and end apart: 5, of which 3 were waited for; matrix products, arithmetic and copies ran while one was open for 0% of the time, Pallas kernels for 3%

profile of v2, /device:TPU:49, one launch (start us, length us, event | category | flops | bytes accessed | tf_op | source)
XLA Modules:
  0.0 59.6 jit_solution(14730059388661587873)
XLA Ops:
  0.6 0.0 copy-start.1
  0.6 0.0 copy-start.2
  0.7 1.0 %copy-done.1 = f32[19,8,8,128]{3,2,1,0:T(8,128)S(1)} copy-done((f32[19,8,8,128]{3,2,1,0:T(8,128)S(1)}, f32[19,8,8,128]{3,2,1,0:T(8,128)}, u32[]{:S(2)}) %copy-start.1) | copy-done | bytes 622616
  1.7 0.0 copy-done.2
  1.8 0.0 copy-done.3
  1.8 0.0 copy-start.11
  1.8 0.4 shard_map.149
  2.2 4.9 %collective-permute-start = (f32[6,8,128]{2,1,0:T(8,128)S(1)}, f32[6,8,128]{2,1,0:T(8,128)S(1)}, u32[]{:S(2)}, u32[]{:S(2)}) collective-permute-start(f32[6,8,128]{2,1,0:T(8,128)S(1)} %get-tuple-element.24), channel_id=1, source_target_pairs={{0,16},{16,32},{32,48},{48,64},{64,80},{80,96},{96,112},{112,128},... | collective-permute-start | bytes 73736 | tf_op jit(solution)/shard_map/ppermute | solution.py:427
  7.1 16.4 %collective-permute-start.1 = (f32[6,8,128]{2,1,0:T(8,128)S(1)}, f32[6,8,128]{2,1,0:T(8,128)S(1)}, u32[]{:S(2)}, u32[]{:S(2)}) collective-permute-start(f32[6,8,128]{2,1,0:T(8,128)S(1)} %get-tuple-element.25), channel_id=1, source_target_pairs={{0,1008},{16,0},{32,16},{48,32},{64,48},{80,64},{96,80},{112,96},{... | collective-permute-start | bytes 73736 | tf_op jit(solution)/shard_map/ppermute | solution.py:427
  23.4 0.0 collective-permute-done.xu_ref
  23.4 0.9 %collective-permute-done.1.xd_ref = f32[6,8,128]{2,1,0:T(8,128)S(1)} collective-permute-done((f32[6,8,128]{2,1,0:T(8,128)S(1)}, f32[6,8,128]{2,1,0:T(8,128)S(1)}, u32[]{:S(2)}, u32[]{:S(2)}) %collective-permute-start.1) | collective-permute-done | bytes 24608 | tf_op jit(solution)/shard_map/ppermute | solution.py:427
  24.4 0.0 copy-start.5
  24.4 4.0 %collective-permute-start.2 = (f32[6,8,128]{2,1,0:T(8,128)S(1)}, f32[6,8,128]{2,1,0:T(8,128)S(1)}, u32[]{:S(2)}, u32[]{:S(2)}) collective-permute-start(f32[6,8,128]{2,1,0:T(8,128)S(1)} %get-tuple-element.28), channel_id=1, source_target_pairs={{0,1},{1,2},{2,3},{3,4},{4,5},{5,6},{6,7},{7,8},{8,9},{9,10},{10,1... | collective-permute-start | bytes 73736 | tf_op jit(solution)/shard_map/ppermute | solution.py:427
  28.4 0.0 collective-permute-start.3
  29.1 0.0 copy-start.9
  29.2 0.6 %copy-done.9 = s32[256]{0:T(256)S(1)} copy-done((s32[256]{0:T(256)S(1)}, s32[256]{0:T(256)}, u32[]{:S(2)}) %copy-start.9) | copy-done | bytes 1048
  29.8 0.9 %shard_map.152 = (f32[16,256]{1,0:T(8,128)S(1)}, f32[16,256]{1,0:T(8,128)S(1)}, f32[8,128]{1,0:T(8,128)S(1)}, bf16[64,256]{1,0:T(8,128)(2,1)S(1)}, bf16[128,256]...) custom-call(f32[1,16,256]{2,1,0:T(8,128)S(1)} %copy-done.5, s32[2,128]{1,0:T(2,128)S(1)} %bitcast.7, ...), custom_call_target="tpu_custom_call" | custom-call | flops 1000000 | bytes 876552 | tf_op jit(solution)/shard_map/pallas_call | solution.py:362
  30.7 0.0 collective-permute-done.2.yu_ref
  30.7 2.2 %collective-permute-done.3.yd_ref = f32[6,8,128]{2,1,0:T(8,128)S(1)} collective-permute-done((f32[6,8,128]{2,1,0:T(8,128)S(1)}, f32[6,8,128]{2,1,0:T(8,128)S(1)}, u32[]{:S(2)}, u32[]{:S(2)}) %collective-permute-start.3) | collective-permute-done | bytes 24608 | tf_op jit(solution)/shard_map/ppermute | solution.py:427
  32.9 1.0 %shard_map.153 = (f32[7,8,8,128]{3,2,1,0:T(8,128)S(1)}, f32[1,256]{1,0:T(1,128)S(1)}, f32[64,8,128]{2,1,0:T(8,128)}) custom-call(f32[7,8,8,128]{3,2,1,0:T(8,128)S(1)} %get-tuple-element.30.heat_post_ref, f32[6,8,128]{2,1,0:T(8,128)S(1)} %collective-permute-done.xu_ref, f32[6,8,128]{2,1,0:T(8,128)S(1)} %collective-permute-done.1.xd_ref, ...), custom_call_target="tpu_custom_call" | custom-call | flops 1000000 | bytes 1020928 | tf_op jit(solution)/shard_map/pallas_call | solution.py:362
  33.9 9.0 %all-to-all-start = ((f32[64,8,128]{2,1,0:T(8,128)}), f32[64,8,128]{2,1,0:T(8,128)S(1)}, u32[]{:S(2)}, u32[]{:S(2)}) async-start(f32[64,8,128]{2,1,0:T(8,128)} %get-tuple-element.34), calls=%async_computation | async-start | bytes 524288 | tf_op jit(solution)/shard_map/all_to_all | solution.py:437
  42.9 1.0 %shard_map.151 = f32[19,8,8,128]{3,2,1,0:T(8,128)} custom-call(f32[19,8,8,128]{3,2,1,0:T(8,128)S(1)} %get-tuple-element.23.post_ref, f32[6,8,128]{2,1,0:T(8,128)S(1)} %collective-permute-done.xu_ref, f32[6,8,128]{2,1,0:T(8,128)S(1)} %collective-permute-done.1.xd_ref, f32[6,8,128]{2,1,0:T(8,128)S(1)} %collective-permute-done.2.yu_ref, ...), custom_call_target="tpu_custom_call" | custom-call | flops 1000000 | bytes 1343488 | tf_op jit(solution)/shard_map/pallas_call | solution.py:362
  43.9 12.1 %all-to-all-done = f32[64,8,128]{2,1,0:T(8,128)S(1)} async-done(((f32[64,8,128]{2,1,0:T(8,128)}), f32[64,8,128]{2,1,0:T(8,128)S(1)}, u32[]{:S(2)}, u32[]{:S(2)}) %all-to-all-start) | async-done | bytes 262176 | tf_op jit(solution)/shard_map/all_to_all | solution.py:437
  56.0 3.7 %shard_map.154 = (f32[7,8,8,128]{3,2,1,0:T(8,128)}, f32[1,16,256]{2,1,0:T(8,128)}) custom-call(f32[512,128]{1,0:T(8,128)S(1)} %bitcast.6, f32[7,8,8,128]{3,2,1,0:T(8,128)S(1)} %get-tuple-element.35.passed_ref, f32[1,256]{1,0:T(1,128)S(1)} %get-tuple-element.36.warmth_ref, bf16[64,256]{1,0:T(8,128)(2,1)S(1)} %get-tuple-element.32.at_plane_ref, ...), custom_call_target="tpu_custom_call" | custom-call | flops 1000000 | bytes 1557508 | tf_op jit(solution)/shard_map/pallas_call | solution.py:362
  (17 shorter events, 0.0 us)
Async XLA Ops:
  0.6 1.1 %copy-start.1 = (f32[19,8,8,128]{3,2,1,0:T(8,128)S(1)}, f32[19,8,8,128]{3,2,1,0:T(8,128)}, u32[]{:S(2)}) copy-start(f32[19,8,8,128]{3,2,1,0:T(8,128)} %flow_ref.1) | copy-start | bytes 1867780
  0.6 1.1 %copy-start.2 = (f32[7,8,8,128]{3,2,1,0:T(8,128)S(1)}, f32[7,8,8,128]{3,2,1,0:T(8,128)}, u32[]{:S(2)}) copy-start(f32[7,8,8,128]{3,2,1,0:T(8,128)} %heat_ref.1) | copy-start | bytes 688132
  0.7 1.1 %copy-start.3 = (s32[8,8,128]{2,1,0:T(8,128)S(1)}, s32[8,8,128]{2,1,0:T(8,128)}, u32[]{:S(2)}) copy-start(s32[8,8,128]{2,1,0:T(8,128)} %mask_ref.1) | copy-start | bytes 98308
  0.7 1.1 %copy-start.4 = (f32[8,8,128]{2,1,0:T(8,128)S(1)}, f32[8,8,128]{2,1,0:T(8,128)}, u32[]{:S(2)}) copy-start(f32[8,8,128]{2,1,0:T(8,128)} %rate_ref.1) | copy-start | bytes 98308
  1.8 27.3 %copy-start = (f32[256,256]{1,0:T(8,128)S(1)}, f32[256,256]{1,0:T(8,128)}, u32[]{:S(2)}) copy-start(f32[256,256]{1,0:T(8,128)} %constant.18.clone.plane_ref) | copy-start | bytes 786436
  1.8 27.3 %copy-start.10 = (s32[256,1]{0,1:T(1,128)S(1)}, s32[256,1]{0,1:T(1,128)}, u32[]{:S(2)}) copy-start(s32[256,1]{0,1:T(1,128)} %param.19) | copy-start | bytes 3076
  1.8 27.4 %copy-start.11 = (s32[256]{0:T(256)S(1)}, s32[256]{0:T(256)}, u32[]{:S(2)}) copy-start(s32[256]{0:T(256)} %param.21) | copy-start | bytes 3076
  2.2 21.3 %collective-permute-start = (f32[6,8,128]{2,1,0:T(8,128)S(1)}, f32[6,8,128]{2,1,0:T(8,128)S(1)}, u32[]{:S(2)}, u32[]{:S(2)}) collective-permute-start(f32[6,8,128]{2,1,0:T(8,128)S(1)} %get-tuple-element.24), channel_id=1, source_target_pairs={{0,16},{16,32},{32,48},{48,64},{64,80},{80,96},{96,112},{112,128},... | collective-permute-start | bytes 73736 | tf_op jit(solution)/shard_map/ppermute | solution.py:427
  7.1 17.3 %collective-permute-start.1 = (f32[6,8,128]{2,1,0:T(8,128)S(1)}, f32[6,8,128]{2,1,0:T(8,128)S(1)}, u32[]{:S(2)}, u32[]{:S(2)}) collective-permute-start(f32[6,8,128]{2,1,0:T(8,128)S(1)} %get-tuple-element.25), channel_id=1, source_target_pairs={{0,1008},{16,0},{32,16},{48,32},{64,48},{80,64},{96,80},{112,96},{... | collective-permute-start | bytes 73736 | tf_op jit(solution)/shard_map/ppermute | solution.py:427
  24.4 4.8 %copy-start.6 = (f32[16,256]{1,0:T(8,128)S(1)}, f32[16,256]{1,0:T(8,128)}, u32[]{:S(2)}) copy-start(f32[16,256]{1,0:T(8,128)} %constant.19.clone.total_ref) | copy-start | bytes 49156
  24.4 4.8 %copy-start.7 = (f32[16,256]{1,0:T(8,128)S(1)}, f32[16,256]{1,0:T(8,128)}, u32[]{:S(2)}) copy-start(f32[16,256]{1,0:T(8,128)} %constant.20.clone.first_ref) | copy-start | bytes 49156
  24.4 4.8 %copy-start.8 = (f32[16,16]{1,0:T(8,128)S(1)}, f32[16,16]{1,0:T(8,128)}, u32[]{:S(2)}) copy-start(f32[16,16]{1,0:T(8,128)} %constant.17.clone.sine_ref) | copy-start | bytes 3076
  24.4 4.8 %copy-start.5 = (f32[1,16,256]{2,1,0:T(8,128)S(1)}, f32[1,16,256]{2,1,0:T(8,128)}, u32[]{:S(2)}) copy-start(f32[1,16,256]{2,1,0:T(8,128)} %source_ref.1) | copy-start | bytes 49156
  24.4 6.3 %collective-permute-start.2 = (f32[6,8,128]{2,1,0:T(8,128)S(1)}, f32[6,8,128]{2,1,0:T(8,128)S(1)}, u32[]{:S(2)}, u32[]{:S(2)}) collective-permute-start(f32[6,8,128]{2,1,0:T(8,128)S(1)} %get-tuple-element.28), channel_id=1, source_target_pairs={{0,1},{1,2},{2,3},{3,4},{4,5},{5,6},{6,7},{7,8},{8,9},{9,10},{10,1... | collective-permute-start | bytes 73736 | tf_op jit(solution)/shard_map/ppermute | solution.py:427
  28.4 4.5 %collective-permute-start.3 = (f32[6,8,128]{2,1,0:T(8,128)S(1)}, f32[6,8,128]{2,1,0:T(8,128)S(1)}, u32[]{:S(2)}, u32[]{:S(2)}) collective-permute-start(f32[6,8,128]{2,1,0:T(8,128)S(1)} %get-tuple-element.29), channel_id=1, source_target_pairs={{0,15},{1,0},{2,1},{3,2},{4,3},{5,4},{6,5},{7,6},{8,7},{9,8},{10,9... | collective-permute-start | bytes 73736 | tf_op jit(solution)/shard_map/ppermute | solution.py:427
  29.1 0.7 %copy-start.9 = (s32[256]{0:T(256)S(1)}, s32[256]{0:T(256)}, u32[]{:S(2)}) copy-start(s32[256]{0:T(256)} %param.20) | copy-start | bytes 3076
  33.9 22.1 %all-to-all-start = ((f32[64,8,128]{2,1,0:T(8,128)}), f32[64,8,128]{2,1,0:T(8,128)S(1)}, u32[]{:S(2)}, u32[]{:S(2)}) async-start(f32[64,8,128]{2,1,0:T(8,128)} %get-tuple-element.34), calls=%async_computation | async-start | bytes 524288 | tf_op jit(solution)/shard_map/all_to_all | solution.py:437

commit v3 on v2

--- a/solution.py
+++ b/solution.py
@@ -41,8 +41,10 @@
 
 x_up = (1, 7, 9, 11, 13)
 x_down = (2, 8, 10, 12, 14)
-y_up = (3, 15, 17, 7, 10)
-y_down = (4, 16, 18, 8, 9)
+y_up = (3, 15, 17)
+y_down = (4, 16, 18)
+diagonal_up = (7, 10)
+diagonal_down = (8, 9)
 
 HIGHEST = lax.Precision.HIGHEST
 limit = 32 * 1024 * 1024
@@ -93,9 +95,9 @@
 
 
 def collide_kernel(
-    flow_ref, heat_ref, mask_ref, rate_ref, _,
-    post_ref, heat_post_ref, xu_ref, xd_ref, yu_ref, yd_ref,
+    flow_ref, heat_ref, mask_ref, rate_ref, *refs
 ):
+    post_ref, heat_post_ref, xu_ref, xd_ref, yu_ref, yd_ref, du_ref, dd_ref = refs[-8:]
     wide_x, wide_y = flow_ref.shape[1], flow_ref.shape[2]
     for x in range(wide_x):
         f = [flow_ref[i, x] for i in range(19)]
@@ -161,6 +163,10 @@
             yu_ref[slot, row, :] = part[last]
         for slot, part in enumerate([heat[4]] + [post[i] for i in y_down]):
             yd_ref[slot, row, :] = part[0:1]
+        for slot, i in enumerate(diagonal_up):
+            du_ref[slot, row, :] = post[i][last]
+        for slot, i in enumerate(diagonal_down):
+            dd_ref[slot, row, :] = post[i][0:1]
 
 
 def block_kernel(
@@ -170,7 +176,7 @@
     *, n_wide, face, depth,
 ):
     sine, plane = sine_ref[...], plane_ref[...]
-    inverse = 1.0 / (total_ref[...] + uptake_ref[0])
+    inverse = 1.0 / (total_ref[...] + uptake_ref[...])
     spectral = dot(dot(sine, source_ref[0], HIGHEST), plane, HIGHEST) * inverse
     cube = dot(dot(sine, spectral, HIGHEST), plane, HIGHEST)
     reply = dot(sine, first_ref[...] * inverse, HIGHEST)
@@ -201,20 +207,17 @@
     return jnp.where(numbers == size - 1, edge, pltpu.roll(rows, size - 1, 0))
 
 
-def rim_kernel(yu_raw_ref, yd_raw_ref, xu_ref, xd_ref, yu_ref, yd_ref):
+def rim_kernel(du_raw_ref, dd_raw_ref, xu_ref, xd_ref, du_ref, dd_ref):
     last = xu_ref.shape[1] - 1
     for raw_ref, out_ref, names, y in (
-        (yu_raw_ref, yu_ref, y_up, last),
-        (yd_raw_ref, yd_ref, y_down, 0),
+        (du_raw_ref, du_ref, diagonal_up, last),
+        (dd_raw_ref, dd_ref, diagonal_down, 0),
     ):
-        out_ref[0] = raw_ref[0]
-        for slot, i in enumerate(names, 1):
+        for slot, i in enumerate(names):
             direction = int(flow_velocity[i, 0])
-            rows = raw_ref[slot]
-            if direction:
-                edges, at = (xu_ref, x_up) if direction > 0 else (xd_ref, x_down)
-                rows = moved_x(rows, direction, edges[1 + at.index(i), y : y + 1, :])
-            out_ref[slot] = rows
+            edges, at = (xu_ref, x_up) if direction > 0 else (xd_ref, x_down)
+            edge = edges[1 + at.index(i), y : y + 1, :]
+            out_ref[slot] = moved_x(raw_ref[slot], direction, edge)
 
 
 def shifted_y(value, direction, edge):
@@ -262,7 +265,7 @@
         send_ref[peer] = message
 
 
-def stream_kernel(post_ref, xu_ref, xd_ref, yu_ref, yd_ref, out_ref):
+def stream_kernel(post_ref, xu_ref, xd_ref, yu_ref, yd_ref, du_ref, dd_ref, out_ref):
     wide_x = post_ref.shape[1]
     for i in range(19):
         cx, cy, cz = (int(c) for c in flow_velocity[i])
@@ -274,8 +277,13 @@
             else:
                 value = post_ref[i, x - cx]
             if cy:
-                edges, at = (yu_ref, y_up) if cy > 0 else (yd_ref, y_down)
-                value = shifted_y(value, cy, edges[1 + at.index(i), x : x + 1, :])
+                if cx:
+                    edges = du_ref if cy > 0 else dd_ref
+                    slot = (diagonal_up if cy > 0 else diagonal_down).index(i)
+                else:
+                    edges = yu_ref if cy > 0 else yd_ref
+                    slot = 1 + (y_up if cy > 0 else y_down).index(i)
+                value = shifted_y(value, cy, edges[slot, x : x + 1, :])
             out_ref[i, x] = shifted_z(value, cz)
 
 
@@ -403,13 +411,15 @@
     (early,) = call(
         first_kernel, (jax.ShapeDtypeStruct((8, nz), jnp.int32),), me, smem=(0,), cost=10**10
     )
-    post, heat_post, xu, xd, yu, yd = call(
+    uptake = cube_uptake_coefficients.reshape(1, 1)
+    post, heat_post, xu, xd, yu, yd, du, dd = call(
         collide_kernel,
         (
             f32(19, bx, by, nz), f32(7, bx, by, nz), f32(6, by, nz), f32(6, by, nz),
-            f32(6, bx, nz), f32(6, bx, nz),
+            f32(4, bx, nz), f32(4, bx, nz), f32(2, bx, nz), f32(2, bx, nz),
         ),
         flow_state, thermal_distributions_current, fluid_mask, heat_rate, early,
+        solid_source, site, owner, node,
     )
     cube, reply, part, at_plane, at_depth, at_owner, at_node = call(
         functools.partial(block_kernel, n_wide=n_wide, face=face, depth=nz),
@@ -417,9 +427,9 @@
             f32(size, face), f32(size, face), f32(8, face // 2),
             b16(bx * by, rows), b16(nz, rows), b16(peers, rows), b16(face, rows),
         ),
-        solid_source, site, owner, node, cube_uptake_coefficients, wide,
-        sine, plane, total, first,
-        smem=(4, 5),
+        solid_source, site, owner, node, uptake, wide, sine, plane, total, first,
+        smem=(5,),
+        cost=10**10,
     )
 
     def send(block, axis, step):
@@ -427,7 +437,6 @@
         return lax.ppermute(block, axis, [(i, (i + step) % count) for i in range(count)])
 
     xu, xd = send(xu, "narrow", 1), send(xd, "narrow", -1)
-    yu, yd = call(rim_kernel, (f32(6, bx, nz), f32(6, bx, nz)), yu, yd, xu, xd)
     yu, yd = send(yu, "wide", 1), send(yd, "wide", -1)
     passed, warmth, message = call(
         warmth_kernel,
@@ -435,7 +444,11 @@
         heat_post, xu, xd, yu, yd, part, at_plane, at_depth,
     )
     got = lax.all_to_all(message, "narrow", split_axis=0, concat_axis=0, tiled=True)
-    (stream,) = call(stream_kernel, (f32(19, bx, by, nz),), post, xu, xd, yu, yd)
+    du, dd = call(rim_kernel, (f32(2, bx, nz), f32(2, bx, nz)), du, dd, xu, xd)
+    du, dd = send(du, "wide", 1), send(dd, "wide", -1)
+    (stream,) = call(
+        stream_kernel, (f32(19, bx, by, nz),), post, xu, xd, yu, yd, du, dd
+    )
     heat, cubes = call(
         functools.partial(finish_kernel, n_wide=n_wide, face=face),
         (f32(7, bx, by, nz), f32(1, size, face)),

time: 59.9 us -> 56 us (0.935)
  starting transfers between devices: 34.3 us -> 31.9 us
  waiting for transfers between devices: 15.3 us -> 14.3 us
  local copies, waits for them, and re-layouts: 1.72 us -> 1.09 us
    all_to_all x1, waiting for transfers between devices: 12.1 us -> 6.99 us  [per_device(): lax.all_to_all(message, 'narrow', split_axis=0, concat_axis=0, tiled=True)]
    ppermute x4 -> x6, waiting for transfers between devices: 3.14 us -> 7.34 us  [send(): lax.ppermute(block, axis, [(i, (i + step) % count) for i in range(count)])]
    all_to_all x1, starting transfers between devices: 9.03 us -> 6.63 us  [per_device(): lax.all_to_all(message, 'narrow', split_axis=0, concat_axis=0, tiled=True)]
    unnamed x24, local copies, waits for them, and re-layouts: 1.72 us -> 1.09 us
    ppermute x4 -> x6, starting transfers between devices: 25.3 us -> 25.3 us  [send(): lax.ppermute(block, axis, [(i, (i + step) % count) for i in range(count)])]
  transfers between devices with their start and end apart: 5 -> 7, of which waited for: 3 -> 4; matrix products, arithmetic and copies ran while one was open for 0% -> 0% of each run, Pallas kernels for 3% -> 3%
where the time goes in v3:
time: 56 us; the launch traced here: 55.7 us
  starting transfers between devices  31.9 us (57%)
  waiting for transfers between devices  14.3 us (26%)
  Pallas kernels  6.87 us (12%)
  between operations  1.5 us (3%)
  local copies, waits for them, and re-layouts  1.09 us (2%)
    ppermute x6, starting transfers between devices, send(): lax.ppermute(block, axis, [(i, (i + step) % count) for i in range(count)])  25.3 us
    ppermute x6, waiting for transfers between devices, send(): lax.ppermute(block, axis, [(i, (i + step) % count) for i in range(count)])  7.34 us
    all_to_all x1, waiting for transfers between devices, per_device(): lax.all_to_all(message, 'narrow', split_axis=0, concat_axis=0, tiled=True)  6.99 us
    pallas_call x7, Pallas kernels, call(): pl.pallas_call(kernel, out_shape=list(shapes), in_specs=[pl.BlockSpec(mem...  6.87 us
    all_to_all x1, starting transfers between devices, per_device(): lax.all_to_all(message, 'narrow', split_axis=0, concat_axis=0, tiled=True)  6.63 us
  transfers between devices with their start and end apart: 7, of which 4 were waited for; matrix products, arithmetic and copies ran while one was open for 0% of the time, Pallas kernels for 3%

profile of v3, /device:TPU:49, one launch (start us, length us, event | category | flops | bytes accessed | tf_op | source)
XLA Modules:
  0.0 55.7 jit_solution(9221885044576444248)
XLA Ops:
  0.7 0.0 copy-start.6
  0.7 1.0 %copy-done = f32[19,8,8,128]{3,2,1,0:T(8,128)S(1)} copy-done((f32[19,8,8,128]{3,2,1,0:T(8,128)S(1)}, f32[19,8,8,128]{3,2,1,0:T(8,128)}, u32[]{:S(2)}) %copy-start) | copy-done | bytes 622616
  1.7 0.0 copy-done.2
  1.8 0.0 copy-start.1
  1.8 0.0 copy-start.10
  1.8 0.0 copy-start.11
  1.8 0.4 shard_map.149
  2.2 0.0 copy-start.9
  2.2 4.9 %collective-permute-start = (f32[6,8,128]{2,1,0:T(8,128)S(1)}, f32[6,8,128]{2,1,0:T(8,128)S(1)}, u32[]{:S(2)}, u32[]{:S(2)}) collective-permute-start(f32[6,8,128]{2,1,0:T(8,128)S(1)} %get-tuple-element.26), channel_id=1, source_target_pairs={{0,16},{16,32},{32,48},{48,64},{64,80},{80,96},{96,112},{112,128},... | collective-permute-start | bytes 73736 | tf_op jit(solution)/shard_map/ppermute | solution.py:437
  7.1 16.4 %collective-permute-start.1 = (f32[6,8,128]{2,1,0:T(8,128)S(1)}, f32[6,8,128]{2,1,0:T(8,128)S(1)}, u32[]{:S(2)}, u32[]{:S(2)}) collective-permute-start(f32[6,8,128]{2,1,0:T(8,128)S(1)} %get-tuple-element.27), channel_id=1, source_target_pairs={{0,1008},{16,0},{32,16},{48,32},{64,48},{80,64},{96,80},{112,96},{... | collective-permute-start | bytes 73736 | tf_op jit(solution)/shard_map/ppermute | solution.py:437
  23.5 3.5 %collective-permute-start.2 = (f32[4,8,128]{2,1,0:T(8,128)S(1)}, f32[4,8,128]{2,1,0:T(8,128)S(1)}, u32[]{:S(2)}, u32[]{:S(2)}) collective-permute-start(f32[4,8,128]{2,1,0:T(8,128)S(1)} %get-tuple-element.28), channel_id=1, source_target_pairs={{0,1},{1,2},{2,3},{3,4},{4,5},{5,6},{6,7},{7,8},{8,9},{9,10},{10,1... | collective-permute-start | bytes 49160 | tf_op jit(solution)/shard_map/ppermute | solution.py:437
  27.0 0.0 collective-permute-start.3
  27.7 0.9 %shard_map.152 = (f32[16,256]{1,0:T(8,128)S(1)}, f32[16,256]{1,0:T(8,128)S(1)}, f32[8,128]{1,0:T(8,128)S(1)}, bf16[64,256]{1,0:T(8,128)(2,1)S(1)}, bf16[128,256]...) custom-call(f32[1,16,256]{2,1,0:T(8,128)S(1)} %copy-done.5, s32[2,128]{1,0:T(2,128)S(1)} %bitcast.10, ...), custom_call_target="tpu_custom_call" | custom-call | flops 10000000000 | bytes 876552 | tf_op jit(solution)/shard_map/pallas_call | solution.py:370
  28.6 0.0 collective-permute-done.2.yu_ref
  28.6 2.8 %collective-permute-done.3.yd_ref = f32[4,8,128]{2,1,0:T(8,128)S(1)} collective-permute-done((f32[4,8,128]{2,1,0:T(8,128)S(1)}, f32[4,8,128]{2,1,0:T(8,128)S(1)}, u32[]{:S(2)}, u32[]{:S(2)}) %collective-permute-start.3) | collective-permute-done | bytes 16416 | tf_op jit(solution)/shard_map/ppermute | solution.py:437
  31.4 1.0 %shard_map.153 = (f32[7,8,8,128]{3,2,1,0:T(8,128)S(1)}, f32[1,256]{1,0:T(1,128)S(1)}, f32[64,8,128]{2,1,0:T(8,128)}) custom-call(f32[7,8,8,128]{3,2,1,0:T(8,128)S(1)} %get-tuple-element.34.heat_post_ref, f32[6,8,128]{2,1,0:T(8,128)S(1)} %collective-permute-done.xu_ref, f32[6,8,128]{2,1,0:T(8,128)S(1)} %collective-permute-done.1.xd_ref, ...), custom_call_target="tpu_custom_call" | custom-call | flops 1000000 | bytes 1004544 | tf_op jit(solution)/shard_map/pallas_call | solution.py:370
  32.3 6.6 %all-to-all-start = ((f32[64,8,128]{2,1,0:T(8,128)}), f32[64,8,128]{2,1,0:T(8,128)S(1)}, u32[]{:S(2)}, u32[]{:S(2)}) async-start(f32[64,8,128]{2,1,0:T(8,128)} %get-tuple-element.38), calls=%async_computation | async-start | bytes 524288 | tf_op jit(solution)/shard_map/all_to_all | solution.py:446
  39.0 0.5 collective-permute-start.4
  39.5 0.0 collective-permute-start.5
  39.5 0.8 %collective-permute-done.4.du_ref = f32[2,8,128]{2,1,0:T(8,128)S(1)} collective-permute-done((f32[2,8,128]{2,1,0:T(8,128)S(1)}, f32[2,8,128]{2,1,0:T(8,128)S(1)}, u32[]{:S(2)}, u32[]{:S(2)}) %collective-permute-start.4) | collective-permute-done | bytes 8224 | tf_op jit(solution)/shard_map/ppermute | solution.py:437
  40.3 3.8 %collective-permute-done.5.dd_ref = f32[2,8,128]{2,1,0:T(8,128)S(1)} collective-permute-done((f32[2,8,128]{2,1,0:T(8,128)S(1)}, f32[2,8,128]{2,1,0:T(8,128)S(1)}, u32[]{:S(2)}, u32[]{:S(2)}) %collective-permute-start.5) | collective-permute-done | bytes 8224 | tf_op jit(solution)/shard_map/ppermute | solution.py:437
  44.1 1.0 %shard_map.151 = f32[19,8,8,128]{3,2,1,0:T(8,128)} custom-call(f32[19,8,8,128]{3,2,1,0:T(8,128)S(1)} %get-tuple-element.25.post_ref, f32[6,8,128]{2,1,0:T(8,128)S(1)} %collective-permute-done.xu_ref, f32[6,8,128]{2,1,0:T(8,128)S(1)} %collective-permute-done.1.xd_ref, f32[4,8,128]{2,1,0:T(8,128)S(1)} %collective-permute-done.2.yu_ref, ...), custom_call_target="tpu_custom_call" | custom-call | flops 1000000 | bytes 1343488 | tf_op jit(solution)/shard_map/pallas_call | solution.py:370
  45.0 7.0 %all-to-all-done = f32[64,8,128]{2,1,0:T(8,128)S(1)} async-done(((f32[64,8,128]{2,1,0:T(8,128)}), f32[64,8,128]{2,1,0:T(8,128)S(1)}, u32[]{:S(2)}, u32[]{:S(2)}) %all-to-all-start) | async-done | bytes 262176 | tf_op jit(solution)/shard_map/all_to_all | solution.py:446
  52.0 3.7 %shard_map.154 = (f32[7,8,8,128]{3,2,1,0:T(8,128)}, f32[1,16,256]{2,1,0:T(8,128)}) custom-call(f32[512,128]{1,0:T(8,128)S(1)} %bitcast.8, f32[7,8,8,128]{3,2,1,0:T(8,128)S(1)} %get-tuple-element.39.passed_ref, f32[1,256]{1,0:T(1,128)S(1)} %get-tuple-element.40.warmth_ref, bf16[64,256]{1,0:T(8,128)(2,1)S(1)} %get-tuple-element.36.at_plane_ref, ...), custom_call_target="tpu_custom_call" | custom-call | flops 1000000 | bytes 1557508 | tf_op jit(solution)/shard_map/pallas_call | solution.py:370
  (21 shorter events, 0.1 us)
Async XLA Ops:
  0.6 1.1 %copy-start = (f32[19,8,8,128]{3,2,1,0:T(8,128)S(1)}, f32[19,8,8,128]{3,2,1,0:T(8,128)}, u32[]{:S(2)}) copy-start(f32[19,8,8,128]{3,2,1,0:T(8,128)} %flow_ref.1) | copy-start | bytes 1867780
  0.6 1.1 %copy-start.2 = (f32[7,8,8,128]{3,2,1,0:T(8,128)S(1)}, f32[7,8,8,128]{3,2,1,0:T(8,128)}, u32[]{:S(2)}) copy-start(f32[7,8,8,128]{3,2,1,0:T(8,128)} %heat_ref.1) | copy-start | bytes 688132
  0.7 1.1 %copy-start.3 = (s32[8,8,128]{2,1,0:T(8,128)S(1)}, s32[8,8,128]{2,1,0:T(8,128)}, u32[]{:S(2)}) copy-start(s32[8,8,128]{2,1,0:T(8,128)} %mask_ref.1) | copy-start | bytes 98308
  0.7 1.1 %copy-start.4 = (f32[8,8,128]{2,1,0:T(8,128)S(1)}, f32[8,8,128]{2,1,0:T(8,128)}, u32[]{:S(2)}) copy-start(f32[8,8,128]{2,1,0:T(8,128)} %rate_ref.1) | copy-start | bytes 98308
  0.7 1.1 %copy-start.5 = (f32[1,16,256]{2,1,0:T(8,128)S(1)}, f32[1,16,256]{2,1,0:T(8,128)}, u32[]{:S(2)}) copy-start(f32[1,16,256]{2,1,0:T(8,128)} %source_ref.1) | copy-start | bytes 49156
  0.7 1.1 %copy-start.7 = (s32[256,1]{0,1:T(1,128)S(1)}, s32[256,1]{0,1:T(1,128)}, u32[]{:S(2)}) copy-start(s32[256,1]{0,1:T(1,128)} %param.19) | copy-start | bytes 3076
  0.7 1.1 %copy-start.8 = (s32[256]{0:T(256)S(1)}, s32[256]{0:T(256)}, u32[]{:S(2)}) copy-start(s32[256]{0:T(256)} %param.21) | copy-start | bytes 3076
  0.7 1.1 %copy-start.6 = (s32[256]{0:T(256)S(1)}, s32[256]{0:T(256)}, u32[]{:S(2)}) copy-start(s32[256]{0:T(256)} %param.20) | copy-start | bytes 3076
  1.8 25.8 %copy-start.1 = (f32[256,256]{1,0:T(8,128)S(1)}, f32[256,256]{1,0:T(8,128)}, u32[]{:S(2)}) copy-start(f32[256,256]{1,0:T(8,128)} %constant.18.clone.plane_ref) | copy-start | bytes 786436
  1.8 25.8 %copy-start.10 = (f32[16,256]{1,0:T(8,128)S(1)}, f32[16,256]{1,0:T(8,128)}, u32[]{:S(2)}) copy-start(f32[16,256]{1,0:T(8,128)} %constant.20.clone.first_ref) | copy-start | bytes 49156
  1.8 25.8 %copy-start.11 = (f32[16,16]{1,0:T(8,128)S(1)}, f32[16,16]{1,0:T(8,128)}, u32[]{:S(2)}) copy-start(f32[16,16]{1,0:T(8,128)} %constant.17.clone.sine_ref) | copy-start | bytes 3076
  2.2 25.5 %copy-start.9 = (f32[16,256]{1,0:T(8,128)S(1)}, f32[16,256]{1,0:T(8,128)}, u32[]{:S(2)}) copy-start(f32[16,256]{1,0:T(8,128)} %constant.19.clone.total_ref) | copy-start | bytes 49156
  2.2 29.1 %collective-permute-start = (f32[6,8,128]{2,1,0:T(8,128)S(1)}, f32[6,8,128]{2,1,0:T(8,128)S(1)}, u32[]{:S(2)}, u32[]{:S(2)}) collective-permute-start(f32[6,8,128]{2,1,0:T(8,128)S(1)} %get-tuple-element.26), channel_id=1, source_target_pairs={{0,16},{16,32},{32,48},{48,64},{64,80},{80,96},{96,112},{112,128},... | collective-permute-start | bytes 73736 | tf_op jit(solution)/shard_map/ppermute | solution.py:437
  7.1 24.2 %collective-permute-start.1 = (f32[6,8,128]{2,1,0:T(8,128)S(1)}, f32[6,8,128]{2,1,0:T(8,128)S(1)}, u32[]{:S(2)}, u32[]{:S(2)}) collective-permute-start(f32[6,8,128]{2,1,0:T(8,128)S(1)} %get-tuple-element.27), channel_id=1, source_target_pairs={{0,1008},{16,0},{32,16},{48,32},{64,48},{80,64},{96,80},{112,96},{... | collective-permute-start | bytes 73736 | tf_op jit(solution)/shard_map/ppermute | solution.py:437
  23.5 5.1 %collective-permute-start.2 = (f32[4,8,128]{2,1,0:T(8,128)S(1)}, f32[4,8,128]{2,1,0:T(8,128)S(1)}, u32[]{:S(2)}, u32[]{:S(2)}) collective-permute-start(f32[4,8,128]{2,1,0:T(8,128)S(1)} %get-tuple-element.28), channel_id=1, source_target_pairs={{0,1},{1,2},{2,3},{3,4},{4,5},{5,6},{6,7},{7,8},{8,9},{9,10},{10,1... | collective-permute-start | bytes 49160 | tf_op jit(solution)/shard_map/ppermute | solution.py:437
  27.0 4.4 %collective-permute-start.3 = (f32[4,8,128]{2,1,0:T(8,128)S(1)}, f32[4,8,128]{2,1,0:T(8,128)S(1)}, u32[]{:S(2)}, u32[]{:S(2)}) collective-permute-start(f32[4,8,128]{2,1,0:T(8,128)S(1)} %get-tuple-element.29), channel_id=1, source_target_pairs={{0,15},{1,0},{2,1},{3,2},{4,3},{5,4},{6,5},{7,6},{8,7},{9,8},{10,9... | collective-permute-start | bytes 49160 | tf_op jit(solution)/shard_map/ppermute | solution.py:437
  32.3 19.7 %all-to-all-start = ((f32[64,8,128]{2,1,0:T(8,128)}), f32[64,8,128]{2,1,0:T(8,128)S(1)}, u32[]{:S(2)}, u32[]{:S(2)}) async-start(f32[64,8,128]{2,1,0:T(8,128)} %get-tuple-element.38), calls=%async_computation | async-start | bytes 524288 | tf_op jit(solution)/shard_map/all_to_all | solution.py:446
  39.0 1.3 %collective-permute-start.4 = (f32[2,8,128]{2,1,0:T(8,128)S(1)}, f32[2,8,128]{2,1,0:T(8,128)S(1)}, u32[]{:S(2)}, u32[]{:S(2)}) collective-permute-start(f32[2,8,128]{2,1,0:T(8,128)S(1)} %get-tuple-element.32), channel_id=1, source_target_pairs={{0,1},{1,2},{2,3},{3,4},{4,5},{5,6},{6,7},{7,8},{8,9},{9,10},{10,1... | collective-permute-start | bytes 24584 | tf_op jit(solution)/shard_map/ppermute | solution.py:437
  39.5 4.6 %collective-permute-start.5 = (f32[2,8,128]{2,1,0:T(8,128)S(1)}, f32[2,8,128]{2,1,0:T(8,128)S(1)}, u32[]{:S(2)}, u32[]{:S(2)}) collective-permute-start(f32[2,8,128]{2,1,0:T(8,128)S(1)} %get-tuple-element.33), channel_id=1, source_target_pairs={{0,15},{1,0},{2,1},{3,2},{4,3},{5,4},{6,5},{7,6},{8,7},{9,8},{10,9... | collective-permute-start | bytes 24584 | tf_op jit(solution)/shard_map/ppermute | solution.py:437

commit v4 on v3

--- a/solution.py
+++ b/solution.py
@@ -57,10 +57,13 @@
     )
     values = 2.0 - 2.0 * np.cos(math.pi * counting / (size + 1))
     plane = np.kron(sine, sine)
+    high = plane.astype(jnp.bfloat16)
+    low = (plane - high.astype(np.float64)).astype(jnp.bfloat16)
+    plane_parts = np.concatenate([high, high, low], axis=0)
     total = values[:, None] + (values[:, None] + values[None, :]).reshape(1, -1)
     return (
         sine.astype(np.float32),
-        plane.astype(np.float32),
+        plane_parts,
         total.astype(np.float32),
         np.ascontiguousarray(np.broadcast_to(sine[:, :1], total.shape)).astype(np.float32),
     )
@@ -94,10 +97,23 @@
     out_ref[...] = jnp.full(out_ref.shape, me_ref[0], jnp.int32)
 
 
-def collide_kernel(
-    flow_ref, heat_ref, mask_ref, rate_ref, *refs
-):
-    post_ref, heat_post_ref, xu_ref, xd_ref, yu_ref, yd_ref, du_ref, dd_ref = refs[-8:]
+def is_odd(me_ref, shape):
+    return jnp.full(shape, me_ref[0] % 2, jnp.int32) == 1
+
+
+def faces_along_x(me_ref, xa_ref, xb_ref):
+    def pick(even_ref, odd_ref):
+        def read(slot, rows=slice(None)):
+            a, b = even_ref[slot, rows, :], odd_ref[slot, rows, :]
+            return jnp.where(is_odd(me_ref, a.shape), b, a)
+
+        return read
+
+    return pick(xa_ref, xb_ref), pick(xb_ref, xa_ref)
+
+
+def collide_kernel(me_ref, flow_ref, heat_ref, mask_ref, rate_ref, *refs):
+    post_ref, heat_post_ref, xa_ref, xb_ref, yu_ref, yd_ref, du_ref, dd_ref = refs[-8:]
     wide_x, wide_y = flow_ref.shape[1], flow_ref.shape[2]
     for x in range(wide_x):
         f = [flow_ref[i, x] for i in range(19)]
@@ -152,12 +168,13 @@
             post_ref[i, x] = post[i]
         for i in range(7):
             heat_post_ref[i, x] = heat[i]
+        if x == 0:
+            down = [heat[2]] + [post[i] for i in x_down]
         if x == wide_x - 1:
-            for slot, part in enumerate([heat[1]] + [post[i] for i in x_up]):
-                xu_ref[slot] = part
-        if x == 0:
-            for slot, part in enumerate([heat[2]] + [post[i] for i in x_down]):
-                xd_ref[slot] = part
+            odd = is_odd(me_ref, heat[1].shape)
+            for slot, (low, high) in enumerate(zip(down, [heat[1]] + [post[i] for i in x_up])):
+                xa_ref[slot] = jnp.where(odd, high, low)
+                xb_ref[slot] = jnp.where(odd, low, high)
         last, row = slice(wide_y - 1, wide_y), slice(x, x + 1)
         for slot, part in enumerate([heat[3]] + [post[i] for i in y_up]):
             yu_ref[slot, row, :] = part[last]
@@ -169,34 +186,52 @@
             dd_ref[slot, row, :] = post[i][0:1]
 
 
-def block_kernel(
+def by_plane(value, parts_ref):
+    high, low = parts_of(value, 2)
+    return dot(jnp.concatenate([high, low, high], axis=1), parts_ref[...])
+
+
+def flat(rows):
+    return jnp.concatenate([rows[0:1], rows[1:2]], axis=1)
+
+
+def face_kernel(
     source_ref, site_ref, owner_ref, node_ref, uptake_ref, wide_ref,
-    sine_ref, plane_ref, total_ref, first_ref,
-    cube_ref, reply_ref, part_ref, at_plane_ref, at_depth_ref, at_owner_ref, at_node_ref,
+    sine_ref, parts_ref, total_ref, first_ref, part_ref, at_plane_ref, at_depth_ref,
     *, n_wide, face, depth,
 ):
-    sine, plane = sine_ref[...], plane_ref[...]
+    first = first_ref[...]
     inverse = 1.0 / (total_ref[...] + uptake_ref[...])
-    spectral = dot(dot(sine, source_ref[0], HIGHEST), plane, HIGHEST) * inverse
-    cube = dot(dot(sine, spectral, HIGHEST), plane, HIGHEST)
-    reply = dot(sine, first_ref[...] * inverse, HIGHEST)
-    cube_ref[...] = cube
-    reply_ref[...] = reply
-    owners, nodes, sites = owner_ref[...], node_ref[...], site_ref[...]
-    number = ((owners * n_wide + wide_ref[0]) * face + nodes).astype(jnp.float32)
+    spectral = by_plane(dot(sine_ref[...], source_ref[0], HIGHEST), parts_ref) * inverse
+    reply = jnp.sum(first * first * inverse, axis=0, keepdims=True)
+    answer = jnp.sum(first * spectral, axis=0, keepdims=True)
+    answer = by_plane(jnp.broadcast_to(answer, (8, face)), parts_ref)[0:1]
+    sites = site_ref[...]
+    number = (owner_ref[...] * n_wide + wide_ref[0]) * face + node_ref[...]
+    number = number.astype(jnp.float32)
     half = face // 2
     part_ref[...] = jnp.concatenate(
         [
-            number, cube[0:1, 0:half], cube[0:1, half:], reply[0:1, 0:half], reply[0:1, half:],
+            number, answer[:, 0:half], answer[:, half:], reply[:, 0:half], reply[:, half:],
             number,
         ],
         axis=0,
     )
-    flat = lambda rows: jnp.concatenate([rows[0:1], rows[1:2]], axis=1)
     at_plane_ref[...] = one_hot(flat(sites // depth), at_plane_ref.shape[0])
     at_depth_ref[...] = one_hot(flat(sites % depth), at_depth_ref.shape[0])
-    at_owner_ref[...] = one_hot(flat(owners), at_owner_ref.shape[0])
-    at_node_ref[...] = one_hot(flat(nodes), at_node_ref.shape[0])
+
+
+def block_kernel(
+    source_ref, owner_ref, node_ref, uptake_ref, sine_ref, parts_ref, total_ref, first_ref, _,
+    cube_ref, reply_ref, at_owner_ref, at_node_ref,
+):
+    sine = sine_ref[...]
+    inverse = 1.0 / (total_ref[...] + uptake_ref[...])
+    spectral = by_plane(dot(sine, source_ref[0], HIGHEST), parts_ref) * inverse
+    cube_ref[...] = by_plane(dot(sine, spectral, HIGHEST), parts_ref)
+    reply_ref[...] = dot(sine, first_ref[...] * inverse, HIGHEST)
+    at_owner_ref[...] = one_hot(flat(owner_ref[...]), at_owner_ref.shape[0])
+    at_node_ref[...] = one_hot(flat(node_ref[...]), at_node_ref.shape[0])
 
 
 def moved_x(rows, direction, edge):
@@ -207,16 +242,17 @@
     return jnp.where(numbers == size - 1, edge, pltpu.roll(rows, size - 1, 0))
 
 
-def rim_kernel(du_raw_ref, dd_raw_ref, xu_ref, xd_ref, du_ref, dd_ref):
-    last = xu_ref.shape[1] - 1
+def rim_kernel(me_ref, du_raw_ref, dd_raw_ref, xa_ref, xb_ref, du_ref, dd_ref):
+    last = xa_ref.shape[1] - 1
+    below, above = faces_along_x(me_ref, xa_ref, xb_ref)
     for raw_ref, out_ref, names, y in (
         (du_raw_ref, du_ref, diagonal_up, last),
         (dd_raw_ref, dd_ref, diagonal_down, 0),
     ):
         for slot, i in enumerate(names):
             direction = int(flow_velocity[i, 0])
-            edges, at = (xu_ref, x_up) if direction > 0 else (xd_ref, x_down)
-            edge = edges[1 + at.index(i), y : y + 1, :]
+            face, at = (below, x_up) if direction > 0 else (above, x_down)
+            edge = face(1 + at.index(i), slice(y, y + 1))
             out_ref[slot] = moved_x(raw_ref[slot], direction, edge)
 
 
@@ -235,16 +271,17 @@
 
 
 def warmth_kernel(
-    heat_post_ref, xu_ref, xd_ref, yu_ref, yd_ref, part_ref, at_plane_ref, at_depth_ref,
+    me_ref, heat_post_ref, xa_ref, yd_ref, yu_ref, xb_ref, part_ref, at_plane_ref, at_depth_ref,
     passed_ref, warmth_ref, send_ref,
 ):
     wide_x, wide_y, depth = heat_post_ref.shape[1:]
+    below, above = faces_along_x(me_ref, xa_ref, xb_ref)
     planes = []
     for x in range(wide_x):
         passed = [
             heat_post_ref[0, x],
-            xu_ref[0] if x == 0 else heat_post_ref[1, x - 1],
-            xd_ref[0] if x == wide_x - 1 else heat_post_ref[2, x + 1],
+            below(0) if x == 0 else heat_post_ref[1, x - 1],
+            above(0) if x == wide_x - 1 else heat_post_ref[2, x + 1],
             shifted_y(heat_post_ref[3, x], 1, yu_ref[0, x : x + 1, :]),
             shifted_y(heat_post_ref[4, x], -1, yd_ref[0, x : x + 1, :]),
             shifted_z(heat_post_ref[5, x], 1),
@@ -265,15 +302,18 @@
         send_ref[peer] = message
 
 
-def stream_kernel(post_ref, xu_ref, xd_ref, yu_ref, yd_ref, du_ref, dd_ref, out_ref):
+def stream_kernel(
+    me_ref, post_ref, xa_ref, yd_ref, yu_ref, xb_ref, dd_ref, du_ref, out_ref
+):
+    below, above = faces_along_x(me_ref, xa_ref, xb_ref)
     wide_x = post_ref.shape[1]
     for i in range(19):
         cx, cy, cz = (int(c) for c in flow_velocity[i])
         for x in range(wide_x):
             if cx > 0 and x == 0:
-                value = xu_ref[1 + x_up.index(i)]
+                value = below(1 + x_up.index(i))
             elif cx < 0 and x == wide_x - 1:
-                value = xd_ref[1 + x_down.index(i)]
+                value = above(1 + x_down.index(i))
             else:
                 value = post_ref[i, x - cx]
             if cy:
@@ -289,7 +329,7 @@
 
 def finish_kernel(
     got_ref, passed_ref, warmth_ref, at_plane_ref, at_depth_ref, at_owner_ref, at_node_ref,
-    me_ref, cube_ref, reply_ref, plane_ref,
+    me_ref, cube_ref, reply_ref, parts_ref,
     heat_ref, cube_out_ref,
     high_ref, low_ref, owner_rows_ref, node_columns_ref, table_ref, *, n_wide, face,
 ):
@@ -336,13 +376,12 @@
                 right.append(jnp.where(hit, one, zero))
         both = both + dot(jnp.concatenate(left, axis=1), jnp.concatenate(right, axis=0))
     table = interface_exchange * (both[0:peers] + both[16 * owner_groups :][0:peers])
-    plane = plane_ref[...]
-    spectral = dot(table, plane, HIGHEST)
+    spectral = by_plane(table, parts_ref)
     table_ref[...] = spectral
     reply = jnp.concatenate([bits(6), bits(7)], axis=1)
     own = table_ref[pl.ds(me_ref[0], 1), :]
-    answers = dot(
-        jnp.concatenate([spectral * reply, reply_ref[...] * own], axis=0), plane, HIGHEST
+    answers = by_plane(
+        jnp.concatenate([spectral * reply, reply_ref[...] * own], axis=0), parts_ref
     )
     surface = answers[0:peers] + jnp.concatenate([bits(4), bits(5)], axis=1)
     cube_out_ref[0] = cube_ref[...] + answers[peers:]
@@ -406,28 +445,26 @@
     node = target_node.reshape(2, rows // 2)
     me = lax.axis_index("narrow").astype(jnp.int32).reshape(1)
     wide = lax.axis_index("wide").astype(jnp.int32).reshape(1)
-    sine, plane, total, first = (jnp.asarray(c) for c in sine_constants(size))
+    sine, plane_parts, total, first = (jnp.asarray(c) for c in sine_constants(size))
 
     (early,) = call(
         first_kernel, (jax.ShapeDtypeStruct((8, nz), jnp.int32),), me, smem=(0,), cost=10**10
     )
     uptake = cube_uptake_coefficients.reshape(1, 1)
-    post, heat_post, xu, xd, yu, yd, du, dd = call(
+    post, heat_post, xa, xb, yu, yd, du, dd = call(
         collide_kernel,
         (
             f32(19, bx, by, nz), f32(7, bx, by, nz), f32(6, by, nz), f32(6, by, nz),
             f32(4, bx, nz), f32(4, bx, nz), f32(2, bx, nz), f32(2, bx, nz),
         ),
-        flow_state, thermal_distributions_current, fluid_mask, heat_rate, early,
+        me, flow_state, thermal_distributions_current, fluid_mask, heat_rate, early,
         solid_source, site, owner, node,
-    )
-    cube, reply, part, at_plane, at_depth, at_owner, at_node = call(
-        functools.partial(block_kernel, n_wide=n_wide, face=face, depth=nz),
-        (
-            f32(size, face), f32(size, face), f32(8, face // 2),
-            b16(bx * by, rows), b16(nz, rows), b16(peers, rows), b16(face, rows),
-        ),
-        solid_source, site, owner, node, uptake, wide, sine, plane, total, first,
+        smem=(0,),
+    )
+    part, at_plane, at_depth = call(
+        functools.partial(face_kernel, n_wide=n_wide, face=face, depth=nz),
+        (f32(8, face // 2), b16(bx * by, rows), b16(nz, rows)),
+        solid_source, site, owner, node, uptake, wide, sine, plane_parts, total, first,
         smem=(5,),
         cost=10**10,
     )
@@ -436,24 +473,36 @@
         count = lax.axis_size(axis)
         return lax.ppermute(block, axis, [(i, (i + step) % count) for i in range(count)])
 
-    xu, xd = send(xu, "narrow", 1), send(xd, "narrow", -1)
-    yu, yd = send(yu, "wide", 1), send(yd, "wide", -1)
+    def swap(block, start):
+        low = range(start, peers, 2)
+        pairs = [(i, (i + 1) % peers) for i in low] + [((i + 1) % peers, i) for i in low]
+        return lax.ppermute(block, "narrow", pairs)
+
+    xa = swap(xa, 1)
+    yd, yu = send(yd, "wide", -1), send(yu, "wide", 1)
+    xb = swap(xb, 0)
     passed, warmth, message = call(
         warmth_kernel,
         (f32(7, bx, by, nz), f32(1, rows), f32(peers, 8, face // 2)),
-        heat_post, xu, xd, yu, yd, part, at_plane, at_depth,
+        me, heat_post, xa, yd, yu, xb, part, at_plane, at_depth,
+        smem=(0,),
     )
     got = lax.all_to_all(message, "narrow", split_axis=0, concat_axis=0, tiled=True)
-    du, dd = call(rim_kernel, (f32(2, bx, nz), f32(2, bx, nz)), du, dd, xu, xd)
-    du, dd = send(du, "wide", 1), send(dd, "wide", -1)
+    du, dd = call(rim_kernel, (f32(2, bx, nz), f32(2, bx, nz)), me, du, dd, xa, xb, smem=(0,))
+    dd, du = send(dd, "wide", -1), send(du, "wide", 1)
     (stream,) = call(
-        stream_kernel, (f32(19, bx, by, nz),), post, xu, xd, yu, yd, du, dd
+        stream_kernel, (f32(19, bx, by, nz),), me, post, xa, yd, yu, xb, dd, du, smem=(0,)
+    )
+    cube, reply, at_owner, at_node = call(
+        block_kernel,
+        (f32(size, face), f32(size, face), b16(peers, rows), b16(face, rows)),
+        solid_source, owner, node, uptake, sine, plane_parts, total, first, du,
     )
     heat, cubes = call(
         functools.partial(finish_kernel, n_wide=n_wide, face=face),
         (f32(7, bx, by, nz), f32(1, size, face)),
         got.reshape(peers * 8, face // 2), passed, warmth, at_plane, at_depth, at_owner, at_node,
-        me, cube, reply, plane,
+        me, cube, reply, plane_parts,
         smem=(7,),
         scratch=[pltpu.VMEM((2, peers, face // 2), jnp.float32)] * 3
         + [pltpu.VMEM((2, face // 2, peers), jnp.float32), pltpu.VMEM((peers, face), jnp.float32)],

time: 56 us -> 53.8 us (0.961)
  waiting for transfers between devices: 14.3 us -> 12 us
    ppermute x0 -> x2, starting transfers between devices: none -> 21.3 us  [swap(): return lax.ppermute(block, 'narrow', pairs)]
    ppermute x6 -> x4, starting transfers between devices: 25.3 us -> 5.51 us  [send(): lax.ppermute(block, axis, [(i, (i + step) % count) for i in range(count)])]
    ppermute x6 -> x4, waiting for transfers between devices: 7.34 us -> 3.92 us  [send(): lax.ppermute(block, axis, [(i, (i + step) % count) for i in range(count)])]
    all_to_all x1, starting transfers between devices: 6.63 us -> 5.18 us  [per_device(): lax.all_to_all(message, 'narrow', split_axis=0, concat_axis=0, tiled=True)]
    ppermute x0 -> x2, waiting for transfers between devices: none -> 1.41 us  [swap(): return lax.ppermute(block, 'narrow', pairs)]
    pallas_call x7 -> x8, Pallas kernels: 6.87 us -> 7.06 us  [call(): pl.pallas_call(kernel, out_shape=list(shapes), in_specs=[pl.BlockSpec(mem...]
  transfers between devices with their start and end apart: 7 -> 7, of which waited for: 4 -> 4; matrix products, arithmetic and copies ran while one was open for 0% -> 0% of each run, Pallas kernels for 3% -> 4%
where the time goes in v4:
time: 53.8 us; the launch traced here: 53.6 us
  starting transfers between devices  31.9 us (59%)
  waiting for transfers between devices  12 us (22%)
  Pallas kernels  7.06 us (13%)
  between operations  1.51 us (3%)
  local copies, waits for them, and re-layouts  1.09 us (2%)
    ppermute x2, starting transfers between devices, swap(): return lax.ppermute(block, 'narrow', pairs)  21.3 us
    pallas_call x8, Pallas kernels, call(): pl.pallas_call(kernel, out_shape=list(shapes), in_specs=[pl.BlockSpec(mem...  7.06 us
    all_to_all x1, waiting for transfers between devices, per_device(): lax.all_to_all(message, 'narrow', split_axis=0, concat_axis=0, tiled=True)  6.62 us
    ppermute x4, starting transfers between devices, send(): lax.ppermute(block, axis, [(i, (i + step) % count) for i in range(count)])  5.51 us
    all_to_all x1, starting transfers between devices, per_device(): lax.all_to_all(message, 'narrow', split_axis=0, concat_axis=0, tiled=True)  5.18 us
    ppermute x4, waiting for transfers between devices, send(): lax.ppermute(block, axis, [(i, (i + step) % count) for i in range(count)])  3.92 us
    ppermute x2, waiting for transfers between devices, swap(): return lax.ppermute(block, 'narrow', pairs)  1.41 us
    unnamed x24, local copies, waits for them, and re-layouts  1.09 us
  transfers between devices with their start and end apart: 7, of which 4 were waited for; matrix products, arithmetic and copies ran while one was open for 0% of the time, Pallas kernels for 4%

profile of v4, /device:TPU:49, one launch (start us, length us, event | category | flops | bytes accessed | tf_op | source)
XLA Modules:
  0.0 53.6 jit_solution(5138010287717665495)
XLA Ops:
  0.7 0.0 copy-start.9
  0.7 1.0 %copy-done.1 = f32[19,8,8,128]{3,2,1,0:T(8,128)S(1)} copy-done((f32[19,8,8,128]{3,2,1,0:T(8,128)S(1)}, f32[19,8,8,128]{3,2,1,0:T(8,128)}, u32[]{:S(2)}) %copy-start.1) | copy-done | bytes 622616
  1.7 0.0 copy-done.2
  1.8 0.0 copy-start
  1.8 0.0 copy-start.7
  1.8 0.0 copy-start.8
  1.8 0.4 shard_map.149
  2.2 0.0 copy-start.6
  2.2 19.3 %collective-permute-start = (f32[6,8,128]{2,1,0:T(8,128)S(1)}, f32[6,8,128]{2,1,0:T(8,128)S(1)}, u32[]{:S(2)}, u32[]{:S(2)}) collective-permute-start(f32[6,8,128]{2,1,0:T(8,128)S(1)} %get-tuple-element.26), channel_id=1, source_target_pairs={{16,32},{48,64},{80,96},{112,128},{144,160},{176,192},{208,224},{2... | collective-permute-start | bytes 73736 | tf_op jit(solution)/shard_map/ppermute | solution.py:479
  21.6 1.0 %collective-permute-start.1 = (f32[4,8,128]{2,1,0:T(8,128)S(1)}, f32[4,8,128]{2,1,0:T(8,128)S(1)}, u32[]{:S(2)}, u32[]{:S(2)}) collective-permute-start(f32[4,8,128]{2,1,0:T(8,128)S(1)} %get-tuple-element.27), channel_id=1, source_target_pairs={{0,15},{1,0},{2,1},{3,2},{4,3},{5,4},{6,5},{7,6},{8,7},{9,8},{10,9... | collective-permute-start | bytes 49160 | tf_op jit(solution)/shard_map/ppermute | solution.py:474
  22.5 2.5 %collective-permute-start.2 = (f32[4,8,128]{2,1,0:T(8,128)S(1)}, f32[4,8,128]{2,1,0:T(8,128)S(1)}, u32[]{:S(2)}, u32[]{:S(2)}) collective-permute-start(f32[4,8,128]{2,1,0:T(8,128)S(1)} %get-tuple-element.28), channel_id=1, source_target_pairs={{0,1},{1,2},{2,3},{3,4},{4,5},{5,6},{6,7},{7,8},{8,9},{9,10},{10,1... | collective-permute-start | bytes 49160 | tf_op jit(solution)/shard_map/ppermute | solution.py:474
  25.1 1.9 %collective-permute-start.3 = (f32[6,8,128]{2,1,0:T(8,128)S(1)}, f32[6,8,128]{2,1,0:T(8,128)S(1)}, u32[]{:S(2)}, u32[]{:S(2)}) collective-permute-start(f32[6,8,128]{2,1,0:T(8,128)S(1)} %get-tuple-element.29), channel_id=1, source_target_pairs={{0,16},{32,48},{64,80},{96,112},{128,144},{160,176},{192,208},{224... | collective-permute-start | bytes 73736 | tf_op jit(solution)/shard_map/ppermute | solution.py:479
  27.7 0.5 shard_map.152
  28.2 0.0 collective-permute-done.2.yu_ref
  28.2 1.4 %collective-permute-done.3.xb_ref = f32[6,8,128]{2,1,0:T(8,128)S(1)} collective-permute-done((f32[6,8,128]{2,1,0:T(8,128)S(1)}, f32[6,8,128]{2,1,0:T(8,128)S(1)}, u32[]{:S(2)}, u32[]{:S(2)}) %collective-permute-start.3) | collective-permute-done | bytes 24608 | tf_op jit(solution)/shard_map/ppermute | solution.py:479
  29.6 1.0 %shard_map.153 = (f32[7,8,8,128]{3,2,1,0:T(8,128)S(1)}, f32[1,256]{1,0:T(1,128)S(1)}, f32[64,8,128]{2,1,0:T(8,128)}) custom-call(s32[1]{0:T(128)} %bitcast.me_ref, f32[7,8,8,128]{3,2,1,0:T(8,128)S(1)} %get-tuple-element.34.heat_post_ref, f32[6,8,128]{2,1,0:T(8,128)S(1)} %collective-permute-done.xa_ref, f32[4,8,128]{2,1,0:T(8,128)S(1)} %collective-permute-done.1.yd_ref, ...), custom_call_target="tpu_custom_call" | custom-call | flops 1000000 | bytes 1004548 | tf_op jit(solution)/shard_map/pallas_call | solution.py:409
  30.6 5.2 %all-to-all-start = ((f32[64,8,128]{2,1,0:T(8,128)}), f32[64,8,128]{2,1,0:T(8,128)S(1)}, u32[]{:S(2)}, u32[]{:S(2)}) async-start(f32[64,8,128]{2,1,0:T(8,128)} %get-tuple-element.38), calls=%async_computation | async-start | bytes 524288 | tf_op jit(solution)/shard_map/all_to_all | solution.py:490
  35.8 2.0 %collective-permute-start.5 = (f32[2,8,128]{2,1,0:T(8,128)S(1)}, f32[2,8,128]{2,1,0:T(8,128)S(1)}, u32[]{:S(2)}, u32[]{:S(2)}) collective-permute-start(f32[2,8,128]{2,1,0:T(8,128)S(1)} %get-tuple-element.33), channel_id=1, source_target_pairs={{0,1},{1,2},{2,3},{3,4},{4,5},{5,6},{6,7},{7,8},{8,9},{9,10},{10,1... | collective-permute-start | bytes 24584 | tf_op jit(solution)/shard_map/ppermute | solution.py:474
  37.8 0.8 %collective-permute-done.5.du_ref._ = f32[2,8,128]{2,1,0:T(8,128)S(1)} collective-permute-done((f32[2,8,128]{2,1,0:T(8,128)S(1)}, f32[2,8,128]{2,1,0:T(8,128)S(1)}, u32[]{:S(2)}, u32[]{:S(2)}) %collective-permute-start.5) | collective-permute-done | bytes 8224 | tf_op jit(solution)/shard_map/ppermute | solution.py:474
  38.6 0.7 %shard_map.154 = (f32[16,256]{1,0:T(8,128)S(1)}, f32[16,256]{1,0:T(8,128)S(1)}, bf16[64,256]{1,0:T(8,128)(2,1)S(1)}, bf16[256,256]{1,0:T(8,128)(2,1)S(1)}) custom-call(f32[1,16,256]{2,1,0:T(8,128)S(1)} %copy-done.3, s32[2,128]{1,0:T(2,128)S(1)} %bitcast.12, s32[2,128]{1,0:T(2,128)S(1)} %bitcast.15, f32[1,1]{1,0:T(1,128)} %bitcast.8.uptake_ref, ...), custom_call_target="tpu_custom_call" | custom-call | flops 1000000 | bytes 1207300 | tf_op jit(solution)/shard_map/pallas_call | solution.py:409
  39.3 3.1 %collective-permute-done.4.dd_ref = f32[2,8,128]{2,1,0:T(8,128)S(1)} collective-permute-done((f32[2,8,128]{2,1,0:T(8,128)S(1)}, f32[2,8,128]{2,1,0:T(8,128)S(1)}, u32[]{:S(2)}, u32[]{:S(2)}) %collective-permute-start.4) | collective-permute-done | bytes 8224 | tf_op jit(solution)/shard_map/ppermute | solution.py:474
  42.4 1.0 %shard_map.151 = f32[19,8,8,128]{3,2,1,0:T(8,128)} custom-call(s32[1]{0:T(128)} %bitcast.me_ref, f32[19,8,8,128]{3,2,1,0:T(8,128)S(1)} %get-tuple-element.25.post_ref, f32[6,8,128]{2,1,0:T(8,128)S(1)} %collective-permute-done.xa_ref, f32[4,8,128]{2,1,0:T(8,128)S(1)} %collective-permute-done.1.yd_ref, f32[4,8,128]{2,1,0:T(8,128)S(1)} %collective-permute-done.2.yu_ref, ...), custom_call_target="tpu_custom_call" | custom-call | flops 1000000 | bytes 1343492 | tf_op jit(solution)/shard_map/pallas_call | solution.py:409
  43.4 6.6 %all-to-all-done = f32[64,8,128]{2,1,0:T(8,128)S(1)} async-done(((f32[64,8,128]{2,1,0:T(8,128)}), f32[64,8,128]{2,1,0:T(8,128)S(1)}, u32[]{:S(2)}, u32[]{:S(2)}) %all-to-all-start) | async-done | bytes 262176 | tf_op jit(solution)/shard_map/all_to_all | solution.py:490
  50.0 3.5 %shard_map.155 = (f32[7,8,8,128]{3,2,1,0:T(8,128)}, f32[1,16,256]{2,1,0:T(8,128)}) custom-call(f32[512,128]{1,0:T(8,128)S(1)} %bitcast.9, f32[7,8,8,128]{3,2,1,0:T(8,128)S(1)} %get-tuple-element.39.passed_ref, f32[1,256]{1,0:T(1,128)S(1)} %get-tuple-element.40.warmth_ref, bf16[64,256]{1,0:T(8,128)(2,1)S(1)} %get-tuple-element.36.at_plane_ref, ...), custom_call_target="tpu_custom_call" | custom-call | flops 1000000 | bytes 2081796 | tf_op jit(solution)/shard_map/pallas_call | solution.py:409
  (22 shorter events, 0.1 us)
Async XLA Ops:
  0.6 1.1 %copy-start.1 = (f32[19,8,8,128]{3,2,1,0:T(8,128)S(1)}, f32[19,8,8,128]{3,2,1,0:T(8,128)}, u32[]{:S(2)}) copy-start(f32[19,8,8,128]{3,2,1,0:T(8,128)} %flow_ref.1) | copy-start | bytes 1867780
  0.6 1.1 %copy-start.2 = (f32[7,8,8,128]{3,2,1,0:T(8,128)S(1)}, f32[7,8,8,128]{3,2,1,0:T(8,128)}, u32[]{:S(2)}) copy-start(f32[7,8,8,128]{3,2,1,0:T(8,128)} %heat_ref.1) | copy-start | bytes 688132
  0.7 1.1 %copy-start.3 = (f32[1,16,256]{2,1,0:T(8,128)S(1)}, f32[1,16,256]{2,1,0:T(8,128)}, u32[]{:S(2)}) copy-start(f32[1,16,256]{2,1,0:T(8,128)} %source_ref.3) | copy-start | bytes 49156
  0.7 1.1 %copy-start.4 = (s32[8,8,128]{2,1,0:T(8,128)S(1)}, s32[8,8,128]{2,1,0:T(8,128)}, u32[]{:S(2)}) copy-start(s32[8,8,128]{2,1,0:T(8,128)} %mask_ref.1) | copy-start | bytes 98308
  0.7 1.1 %copy-start.5 = (f32[8,8,128]{2,1,0:T(8,128)S(1)}, f32[8,8,128]{2,1,0:T(8,128)}, u32[]{:S(2)}) copy-start(f32[8,8,128]{2,1,0:T(8,128)} %rate_ref.1) | copy-start | bytes 98308
  0.7 1.1 %copy-start.10 = (s32[256]{0:T(256)S(1)}, s32[256]{0:T(256)}, u32[]{:S(2)}) copy-start(s32[256]{0:T(256)} %param.21) | copy-start | bytes 3076
  0.7 1.1 %copy-start.11 = (s32[256]{0:T(256)S(1)}, s32[256]{0:T(256)}, u32[]{:S(2)}) copy-start(s32[256]{0:T(256)} %param.20) | copy-start | bytes 3076
  0.7 1.1 %copy-start.9 = (s32[256,1]{0,1:T(1,128)S(1)}, s32[256,1]{0,1:T(1,128)}, u32[]{:S(2)}) copy-start(s32[256,1]{0,1:T(1,128)} %param.19) | copy-start | bytes 3076
  1.8 25.9 %copy-start = (bf16[768,256]{1,0:T(8,128)(2,1)S(1)}, bf16[768,256]{1,0:T(8,128)(2,1)}, u32[]{:S(2)}) copy-start(bf16[768,256]{1,0:T(8,128)(2,1)} %constant.18.clone.parts_ref) | copy-start | bytes 1179652
  1.8 25.8 %copy-start.7 = (f32[16,256]{1,0:T(8,128)S(1)}, f32[16,256]{1,0:T(8,128)}, u32[]{:S(2)}) copy-start(f32[16,256]{1,0:T(8,128)} %constant.20.clone.first_ref) | copy-start | bytes 49156
  1.8 25.8 %copy-start.8 = (f32[16,16]{1,0:T(8,128)S(1)}, f32[16,16]{1,0:T(8,128)}, u32[]{:S(2)}) copy-start(f32[16,16]{1,0:T(8,128)} %constant.17.clone.sine_ref) | copy-start | bytes 3076
  2.2 25.5 %copy-start.6 = (f32[16,256]{1,0:T(8,128)S(1)}, f32[16,256]{1,0:T(8,128)}, u32[]{:S(2)}) copy-start(f32[16,256]{1,0:T(8,128)} %constant.19.clone.total_ref) | copy-start | bytes 49156
  2.2 26.0 %collective-permute-start = (f32[6,8,128]{2,1,0:T(8,128)S(1)}, f32[6,8,128]{2,1,0:T(8,128)S(1)}, u32[]{:S(2)}, u32[]{:S(2)}) collective-permute-start(f32[6,8,128]{2,1,0:T(8,128)S(1)} %get-tuple-element.26), channel_id=1, source_target_pairs={{16,32},{48,64},{80,96},{112,128},{144,160},{176,192},{208,224},{2... | collective-permute-start | bytes 73736 | tf_op jit(solution)/shard_map/ppermute | solution.py:479
  21.6 6.6 %collective-permute-start.1 = (f32[4,8,128]{2,1,0:T(8,128)S(1)}, f32[4,8,128]{2,1,0:T(8,128)S(1)}, u32[]{:S(2)}, u32[]{:S(2)}) collective-permute-start(f32[4,8,128]{2,1,0:T(8,128)S(1)} %get-tuple-element.27), channel_id=1, source_target_pairs={{0,15},{1,0},{2,1},{3,2},{4,3},{5,4},{6,5},{7,6},{8,7},{9,8},{10,9... | collective-permute-start | bytes 49160 | tf_op jit(solution)/shard_map/ppermute | solution.py:474
  22.5 5.7 %collective-permute-start.2 = (f32[4,8,128]{2,1,0:T(8,128)S(1)}, f32[4,8,128]{2,1,0:T(8,128)S(1)}, u32[]{:S(2)}, u32[]{:S(2)}) collective-permute-start(f32[4,8,128]{2,1,0:T(8,128)S(1)} %get-tuple-element.28), channel_id=1, source_target_pairs={{0,1},{1,2},{2,3},{3,4},{4,5},{5,6},{6,7},{7,8},{8,9},{9,10},{10,1... | collective-permute-start | bytes 49160 | tf_op jit(solution)/shard_map/ppermute | solution.py:474
  25.1 4.6 %collective-permute-start.3 = (f32[6,8,128]{2,1,0:T(8,128)S(1)}, f32[6,8,128]{2,1,0:T(8,128)S(1)}, u32[]{:S(2)}, u32[]{:S(2)}) collective-permute-start(f32[6,8,128]{2,1,0:T(8,128)S(1)} %get-tuple-element.29), channel_id=1, source_target_pairs={{0,16},{32,48},{64,80},{96,112},{128,144},{160,176},{192,208},{224... | collective-permute-start | bytes 73736 | tf_op jit(solution)/shard_map/ppermute | solution.py:479
  30.6 19.4 %all-to-all-start = ((f32[64,8,128]{2,1,0:T(8,128)}), f32[64,8,128]{2,1,0:T(8,128)S(1)}, u32[]{:S(2)}, u32[]{:S(2)}) async-start(f32[64,8,128]{2,1,0:T(8,128)} %get-tuple-element.38), calls=%async_computation | async-start | bytes 524288 | tf_op jit(solution)/shard_map/all_to_all | solution.py:490
  35.8 2.8 %collective-permute-start.5 = (f32[2,8,128]{2,1,0:T(8,128)S(1)}, f32[2,8,128]{2,1,0:T(8,128)S(1)}, u32[]{:S(2)}, u32[]{:S(2)}) collective-permute-start(f32[2,8,128]{2,1,0:T(8,128)S(1)} %get-tuple-element.33), channel_id=1, source_target_pairs={{0,1},{1,2},{2,3},{3,4},{4,5},{5,6},{6,7},{7,8},{8,9},{9,10},{10,1... | collective-permute-start | bytes 24584 | tf_op jit(solution)/shard_map/ppermute | solution.py:474
  37.8 4.6 %collective-permute-start.4 = (f32[2,8,128]{2,1,0:T(8,128)S(1)}, f32[2,8,128]{2,1,0:T(8,128)S(1)}, u32[]{:S(2)}, u32[]{:S(2)}) collective-permute-start(f32[2,8,128]{2,1,0:T(8,128)S(1)} %get-tuple-element.32), channel_id=1, source_target_pairs={{0,15},{1,0},{2,1},{3,2},{4,3},{5,4},{6,5},{7,6},{8,7},{9,8},{10,9... | collective-permute-start | bytes 24584 | tf_op jit(solution)/shard_map/ppermute | solution.py:474

commit v5 on v4

--- a/solution.py
+++ b/solution.py
@@ -126,8 +126,7 @@
                 functools.reduce(lambda a, b: a + b, plus)
                 - functools.reduce(lambda a, b: a + b, minus)
             )
-        inverse = 1.0 / density
-        speed = [m * inverse for m in momentum]
+        speed = [m / density for m in momentum]
         square = speed[0] * speed[0] + speed[1] * speed[1] + speed[2] * speed[2]
         base = 1.0 - 1.5 * square
         is_fluid = mask_ref[x] == 1

time: 53.8 us -> 53.8 us (level)
  no operation moved by 1% of the time
where the time goes in v5:
time: 53.8 us; the launch traced here: 53.6 us
  starting transfers between devices  31.9 us (59%)
  waiting for transfers between devices  12 us (22%)
  Pallas kernels  7.06 us (13%)
  between operations  1.51 us (3%)
  local copies, waits for them, and re-layouts  1.09 us (2%)
    ppermute x2, starting transfers between devices, swap(): return lax.ppermute(block, 'narrow', pairs)  21.3 us
    pallas_call x8, Pallas kernels, call(): pl.pallas_call(kernel, out_shape=list(shapes), in_specs=[pl.BlockSpec(mem...  7.06 us
    all_to_all x1, waiting for transfers between devices, per_device(): lax.all_to_all(message, 'narrow', split_axis=0, concat_axis=0, tiled=True)  6.62 us
    ppermute x4, starting transfers between devices, send(): lax.ppermute(block, axis, [(i, (i + step) % count) for i in range(count)])  5.51 us
    all_to_all x1, starting transfers between devices, per_device(): lax.all_to_all(message, 'narrow', split_axis=0, concat_axis=0, tiled=True)  5.18 us
    ppermute x4, waiting for transfers between devices, send(): lax.ppermute(block, axis, [(i, (i + step) % count) for i in range(count)])  3.92 us
    ppermute x2, waiting for transfers between devices, swap(): return lax.ppermute(block, 'narrow', pairs)  1.41 us
    unnamed x24, local copies, waits for them, and re-layouts  1.09 us
  transfers between devices with their start and end apart: 7, of which 4 were waited for; matrix products, arithmetic and copies ran while one was open for 0% of the time, Pallas kernels for 4%

profile of v5, /device:TPU:49, one launch (start us, length us, event | category | flops | bytes accessed | tf_op | source)
XLA Modules:
  0.0 53.6 jit_solution(5138010287717665495)
XLA Ops:
  0.7 0.0 copy-start.9
  0.7 1.0 %copy-done.1 = f32[19,8,8,128]{3,2,1,0:T(8,128)S(1)} copy-done((f32[19,8,8,128]{3,2,1,0:T(8,128)S(1)}, f32[19,8,8,128]{3,2,1,0:T(8,128)}, u32[]{:S(2)}) %copy-start.1) | copy-done | bytes 622616
  1.7 0.0 copy-done.2
  1.8 0.0 copy-start
  1.8 0.0 copy-start.7
  1.8 0.0 copy-start.8
  1.8 0.4 shard_map.149
  2.2 0.0 copy-start.6
  2.2 19.3 %collective-permute-start = (f32[6,8,128]{2,1,0:T(8,128)S(1)}, f32[6,8,128]{2,1,0:T(8,128)S(1)}, u32[]{:S(2)}, u32[]{:S(2)}) collective-permute-start(f32[6,8,128]{2,1,0:T(8,128)S(1)} %get-tuple-element.26), channel_id=1, source_target_pairs={{16,32},{48,64},{80,96},{112,128},{144,160},{176,192},{208,224},{2... | collective-permute-start | bytes 73736 | tf_op jit(solution)/shard_map/ppermute | solution.py:478
  21.6 1.0 %collective-permute-start.1 = (f32[4,8,128]{2,1,0:T(8,128)S(1)}, f32[4,8,128]{2,1,0:T(8,128)S(1)}, u32[]{:S(2)}, u32[]{:S(2)}) collective-permute-start(f32[4,8,128]{2,1,0:T(8,128)S(1)} %get-tuple-element.27), channel_id=1, source_target_pairs={{0,15},{1,0},{2,1},{3,2},{4,3},{5,4},{6,5},{7,6},{8,7},{9,8},{10,9... | collective-permute-start | bytes 49160 | tf_op jit(solution)/shard_map/ppermute | solution.py:473
  22.5 2.5 %collective-permute-start.2 = (f32[4,8,128]{2,1,0:T(8,128)S(1)}, f32[4,8,128]{2,1,0:T(8,128)S(1)}, u32[]{:S(2)}, u32[]{:S(2)}) collective-permute-start(f32[4,8,128]{2,1,0:T(8,128)S(1)} %get-tuple-element.28), channel_id=1, source_target_pairs={{0,1},{1,2},{2,3},{3,4},{4,5},{5,6},{6,7},{7,8},{8,9},{9,10},{10,1... | collective-permute-start | bytes 49160 | tf_op jit(solution)/shard_map/ppermute | solution.py:473
  25.1 1.9 %collective-permute-start.3 = (f32[6,8,128]{2,1,0:T(8,128)S(1)}, f32[6,8,128]{2,1,0:T(8,128)S(1)}, u32[]{:S(2)}, u32[]{:S(2)}) collective-permute-start(f32[6,8,128]{2,1,0:T(8,128)S(1)} %get-tuple-element.29), channel_id=1, source_target_pairs={{0,16},{32,48},{64,80},{96,112},{128,144},{160,176},{192,208},{224... | collective-permute-start | bytes 73736 | tf_op jit(solution)/shard_map/ppermute | solution.py:478
  27.7 0.5 shard_map.152
  28.2 0.0 collective-permute-done.2.yu_ref
  28.2 1.4 %collective-permute-done.3.xb_ref = f32[6,8,128]{2,1,0:T(8,128)S(1)} collective-permute-done((f32[6,8,128]{2,1,0:T(8,128)S(1)}, f32[6,8,128]{2,1,0:T(8,128)S(1)}, u32[]{:S(2)}, u32[]{:S(2)}) %collective-permute-start.3) | collective-permute-done | bytes 24608 | tf_op jit(solution)/shard_map/ppermute | solution.py:478
  29.6 1.0 %shard_map.153 = (f32[7,8,8,128]{3,2,1,0:T(8,128)S(1)}, f32[1,256]{1,0:T(1,128)S(1)}, f32[64,8,128]{2,1,0:T(8,128)}) custom-call(s32[1]{0:T(128)} %bitcast.me_ref, f32[7,8,8,128]{3,2,1,0:T(8,128)S(1)} %get-tuple-element.34.heat_post_ref, f32[6,8,128]{2,1,0:T(8,128)S(1)} %collective-permute-done.xa_ref, f32[4,8,128]{2,1,0:T(8,128)S(1)} %collective-permute-done.1.yd_ref, ...), custom_call_target="tpu_custom_call" | custom-call | flops 1000000 | bytes 1004548 | tf_op jit(solution)/shard_map/pallas_call | solution.py:408
  30.6 5.2 %all-to-all-start = ((f32[64,8,128]{2,1,0:T(8,128)}), f32[64,8,128]{2,1,0:T(8,128)S(1)}, u32[]{:S(2)}, u32[]{:S(2)}) async-start(f32[64,8,128]{2,1,0:T(8,128)} %get-tuple-element.38), calls=%async_computation | async-start | bytes 524288 | tf_op jit(solution)/shard_map/all_to_all | solution.py:489
  35.8 2.0 %collective-permute-start.5 = (f32[2,8,128]{2,1,0:T(8,128)S(1)}, f32[2,8,128]{2,1,0:T(8,128)S(1)}, u32[]{:S(2)}, u32[]{:S(2)}) collective-permute-start(f32[2,8,128]{2,1,0:T(8,128)S(1)} %get-tuple-element.33), channel_id=1, source_target_pairs={{0,1},{1,2},{2,3},{3,4},{4,5},{5,6},{6,7},{7,8},{8,9},{9,10},{10,1... | collective-permute-start | bytes 24584 | tf_op jit(solution)/shard_map/ppermute | solution.py:473
  37.8 0.8 %collective-permute-done.5.du_ref._ = f32[2,8,128]{2,1,0:T(8,128)S(1)} collective-permute-done((f32[2,8,128]{2,1,0:T(8,128)S(1)}, f32[2,8,128]{2,1,0:T(8,128)S(1)}, u32[]{:S(2)}, u32[]{:S(2)}) %collective-permute-start.5) | collective-permute-done | bytes 8224 | tf_op jit(solution)/shard_map/ppermute | solution.py:473
  38.6 0.7 %shard_map.154 = (f32[16,256]{1,0:T(8,128)S(1)}, f32[16,256]{1,0:T(8,128)S(1)}, bf16[64,256]{1,0:T(8,128)(2,1)S(1)}, bf16[256,256]{1,0:T(8,128)(2,1)S(1)}) custom-call(f32[1,16,256]{2,1,0:T(8,128)S(1)} %copy-done.3, s32[2,128]{1,0:T(2,128)S(1)} %bitcast.12, s32[2,128]{1,0:T(2,128)S(1)} %bitcast.15, f32[1,1]{1,0:T(1,128)} %bitcast.8.uptake_ref, ...), custom_call_target="tpu_custom_call" | custom-call | flops 1000000 | bytes 1207300 | tf_op jit(solution)/shard_map/pallas_call | solution.py:408
  39.3 3.1 %collective-permute-done.4.dd_ref = f32[2,8,128]{2,1,0:T(8,128)S(1)} collective-permute-done((f32[2,8,128]{2,1,0:T(8,128)S(1)}, f32[2,8,128]{2,1,0:T(8,128)S(1)}, u32[]{:S(2)}, u32[]{:S(2)}) %collective-permute-start.4) | collective-permute-done | bytes 8224 | tf_op jit(solution)/shard_map/ppermute | solution.py:473
  42.4 1.0 %shard_map.151 = f32[19,8,8,128]{3,2,1,0:T(8,128)} custom-call(s32[1]{0:T(128)} %bitcast.me_ref, f32[19,8,8,128]{3,2,1,0:T(8,128)S(1)} %get-tuple-element.25.post_ref, f32[6,8,128]{2,1,0:T(8,128)S(1)} %collective-permute-done.xa_ref, f32[4,8,128]{2,1,0:T(8,128)S(1)} %collective-permute-done.1.yd_ref, f32[4,8,128]{2,1,0:T(8,128)S(1)} %collective-permute-done.2.yu_ref, ...), custom_call_target="tpu_custom_call" | custom-call | flops 1000000 | bytes 1343492 | tf_op jit(solution)/shard_map/pallas_call | solution.py:408
  43.4 6.6 %all-to-all-done = f32[64,8,128]{2,1,0:T(8,128)S(1)} async-done(((f32[64,8,128]{2,1,0:T(8,128)}), f32[64,8,128]{2,1,0:T(8,128)S(1)}, u32[]{:S(2)}, u32[]{:S(2)}) %all-to-all-start) | async-done | bytes 262176 | tf_op jit(solution)/shard_map/all_to_all | solution.py:489
  50.0 3.5 %shard_map.155 = (f32[7,8,8,128]{3,2,1,0:T(8,128)}, f32[1,16,256]{2,1,0:T(8,128)}) custom-call(f32[512,128]{1,0:T(8,128)S(1)} %bitcast.9, f32[7,8,8,128]{3,2,1,0:T(8,128)S(1)} %get-tuple-element.39.passed_ref, f32[1,256]{1,0:T(1,128)S(1)} %get-tuple-element.40.warmth_ref, bf16[64,256]{1,0:T(8,128)(2,1)S(1)} %get-tuple-element.36.at_plane_ref, ...), custom_call_target="tpu_custom_call" | custom-call | flops 1000000 | bytes 2081796 | tf_op jit(solution)/shard_map/pallas_call | solution.py:408
  (22 shorter events, 0.1 us)
Async XLA Ops:
  0.6 1.1 %copy-start.1 = (f32[19,8,8,128]{3,2,1,0:T(8,128)S(1)}, f32[19,8,8,128]{3,2,1,0:T(8,128)}, u32[]{:S(2)}) copy-start(f32[19,8,8,128]{3,2,1,0:T(8,128)} %flow_ref.1) | copy-start | bytes 1867780
  0.6 1.1 %copy-start.2 = (f32[7,8,8,128]{3,2,1,0:T(8,128)S(1)}, f32[7,8,8,128]{3,2,1,0:T(8,128)}, u32[]{:S(2)}) copy-start(f32[7,8,8,128]{3,2,1,0:T(8,128)} %heat_ref.1) | copy-start | bytes 688132
  0.7 1.1 %copy-start.3 = (f32[1,16,256]{2,1,0:T(8,128)S(1)}, f32[1,16,256]{2,1,0:T(8,128)}, u32[]{:S(2)}) copy-start(f32[1,16,256]{2,1,0:T(8,128)} %source_ref.3) | copy-start | bytes 49156
  0.7 1.1 %copy-start.4 = (s32[8,8,128]{2,1,0:T(8,128)S(1)}, s32[8,8,128]{2,1,0:T(8,128)}, u32[]{:S(2)}) copy-start(s32[8,8,128]{2,1,0:T(8,128)} %mask_ref.1) | copy-start | bytes 98308
  0.7 1.1 %copy-start.5 = (f32[8,8,128]{2,1,0:T(8,128)S(1)}, f32[8,8,128]{2,1,0:T(8,128)}, u32[]{:S(2)}) copy-start(f32[8,8,128]{2,1,0:T(8,128)} %rate_ref.1) | copy-start | bytes 98308
  0.7 1.1 %copy-start.10 = (s32[256]{0:T(256)S(1)}, s32[256]{0:T(256)}, u32[]{:S(2)}) copy-start(s32[256]{0:T(256)} %param.21) | copy-start | bytes 3076
  0.7 1.1 %copy-start.11 = (s32[256]{0:T(256)S(1)}, s32[256]{0:T(256)}, u32[]{:S(2)}) copy-start(s32[256]{0:T(256)} %param.20) | copy-start | bytes 3076
  0.7 1.1 %copy-start.9 = (s32[256,1]{0,1:T(1,128)S(1)}, s32[256,1]{0,1:T(1,128)}, u32[]{:S(2)}) copy-start(s32[256,1]{0,1:T(1,128)} %param.19) | copy-start | bytes 3076
  1.8 25.9 %copy-start = (bf16[768,256]{1,0:T(8,128)(2,1)S(1)}, bf16[768,256]{1,0:T(8,128)(2,1)}, u32[]{:S(2)}) copy-start(bf16[768,256]{1,0:T(8,128)(2,1)} %constant.18.clone.parts_ref) | copy-start | bytes 1179652
  1.8 25.8 %copy-start.7 = (f32[16,256]{1,0:T(8,128)S(1)}, f32[16,256]{1,0:T(8,128)}, u32[]{:S(2)}) copy-start(f32[16,256]{1,0:T(8,128)} %constant.20.clone.first_ref) | copy-start | bytes 49156
  1.8 25.8 %copy-start.8 = (f32[16,16]{1,0:T(8,128)S(1)}, f32[16,16]{1,0:T(8,128)}, u32[]{:S(2)}) copy-start(f32[16,16]{1,0:T(8,128)} %constant.17.clone.sine_ref) | copy-start | bytes 3076
  2.2 25.5 %copy-start.6 = (f32[16,256]{1,0:T(8,128)S(1)}, f32[16,256]{1,0:T(8,128)}, u32[]{:S(2)}) copy-start(f32[16,256]{1,0:T(8,128)} %constant.19.clone.total_ref) | copy-start | bytes 49156
  2.2 26.0 %collective-permute-start = (f32[6,8,128]{2,1,0:T(8,128)S(1)}, f32[6,8,128]{2,1,0:T(8,128)S(1)}, u32[]{:S(2)}, u32[]{:S(2)}) collective-permute-start(f32[6,8,128]{2,1,0:T(8,128)S(1)} %get-tuple-element.26), channel_id=1, source_target_pairs={{16,32},{48,64},{80,96},{112,128},{144,160},{176,192},{208,224},{2... | collective-permute-start | bytes 73736 | tf_op jit(solution)/shard_map/ppermute | solution.py:478
  21.6 6.6 %collective-permute-start.1 = (f32[4,8,128]{2,1,0:T(8,128)S(1)}, f32[4,8,128]{2,1,0:T(8,128)S(1)}, u32[]{:S(2)}, u32[]{:S(2)}) collective-permute-start(f32[4,8,128]{2,1,0:T(8,128)S(1)} %get-tuple-element.27), channel_id=1, source_target_pairs={{0,15},{1,0},{2,1},{3,2},{4,3},{5,4},{6,5},{7,6},{8,7},{9,8},{10,9... | collective-permute-start | bytes 49160 | tf_op jit(solution)/shard_map/ppermute | solution.py:473
  22.5 5.7 %collective-permute-start.2 = (f32[4,8,128]{2,1,0:T(8,128)S(1)}, f32[4,8,128]{2,1,0:T(8,128)S(1)}, u32[]{:S(2)}, u32[]{:S(2)}) collective-permute-start(f32[4,8,128]{2,1,0:T(8,128)S(1)} %get-tuple-element.28), channel_id=1, source_target_pairs={{0,1},{1,2},{2,3},{3,4},{4,5},{5,6},{6,7},{7,8},{8,9},{9,10},{10,1... | collective-permute-start | bytes 49160 | tf_op jit(solution)/shard_map/ppermute | solution.py:473
  25.1 4.6 %collective-permute-start.3 = (f32[6,8,128]{2,1,0:T(8,128)S(1)}, f32[6,8,128]{2,1,0:T(8,128)S(1)}, u32[]{:S(2)}, u32[]{:S(2)}) collective-permute-start(f32[6,8,128]{2,1,0:T(8,128)S(1)} %get-tuple-element.29), channel_id=1, source_target_pairs={{0,16},{32,48},{64,80},{96,112},{128,144},{160,176},{192,208},{224... | collective-permute-start | bytes 73736 | tf_op jit(solution)/shard_map/ppermute | solution.py:478
  30.6 19.4 %all-to-all-start = ((f32[64,8,128]{2,1,0:T(8,128)}), f32[64,8,128]{2,1,0:T(8,128)S(1)}, u32[]{:S(2)}, u32[]{:S(2)}) async-start(f32[64,8,128]{2,1,0:T(8,128)} %get-tuple-element.38), calls=%async_computation | async-start | bytes 524288 | tf_op jit(solution)/shard_map/all_to_all | solution.py:489
  35.8 2.8 %collective-permute-start.5 = (f32[2,8,128]{2,1,0:T(8,128)S(1)}, f32[2,8,128]{2,1,0:T(8,128)S(1)}, u32[]{:S(2)}, u32[]{:S(2)}) collective-permute-start(f32[2,8,128]{2,1,0:T(8,128)S(1)} %get-tuple-element.33), channel_id=1, source_target_pairs={{0,1},{1,2},{2,3},{3,4},{4,5},{5,6},{6,7},{7,8},{8,9},{9,10},{10,1... | collective-permute-start | bytes 24584 | tf_op jit(solution)/shard_map/ppermute | solution.py:473
  37.8 4.6 %collective-permute-start.4 = (f32[2,8,128]{2,1,0:T(8,128)S(1)}, f32[2,8,128]{2,1,0:T(8,128)S(1)}, u32[]{:S(2)}, u32[]{:S(2)}) collective-permute-start(f32[2,8,128]{2,1,0:T(8,128)S(1)} %get-tuple-element.32), channel_id=1, source_target_pairs={{0,15},{1,0},{2,1},{3,2},{4,3},{5,4},{6,5},{7,6},{8,7},{9,8},{10,9... | collective-permute-start | bytes 24584 | tf_op jit(solution)/shard_map/ppermute | solution.py:473
